TPU v7x, 32 devices: a whole 2x2x4 slice. The times are simulated.
32 devices in a mesh: seq: 8 (over z, y), chan: 4 (over x, core).
Axes of the slice: x: 2, y: 2, z: 4, core: 2. Of those that a mesh axis runs over, the one named last changes fastest.
Arguments:
- features: bfloat16 [4096, 512], P('seq', 'chan'), may hold values from -600 to 600
- pre_gate: bfloat16 [4096, 512], P('seq', 'chan'), may hold values from -6 to 6
- post_gate: bfloat16 [4096, 512], P('seq', 'chan'), may hold values from -6 to 6
- norm_gain: float32 [512], P('chan'), may hold values from 0.1 to 1.9
- skip_weight: float32 [512], P('chan'), may hold values from -4 to 4
- spectrum: float32 [2, 16, 512, 512], P(None, 'seq', None, 'chan'), may hold values from -6 to 6
Outputs:
- gated_out: bfloat16 [4096, 512], P('seq', 'chan')
All inputs are finite; a program needn't handle non-finite values.
Results may differ from a plain program's by a relative error of at most 0.007.
Values may be sent and summed in bfloat16 or wider, within the bound.
No kernel may reach another device: no remote copies, remote signals or barrier semaphores. Data moves between devices by JAX's collectives and lax.ppermute only.
A program may use at most 64 MiB of HBM per device.

v0:
```python
import functools

import jax
import jax.numpy as jnp
import numpy as np
from jax import lax
from jax.experimental import pallas as pl
from jax.experimental.pallas import tpu as pltpu
from jax.sharding import PartitionSpec as P

EPS = 1e-06
BF16 = jnp.bfloat16
F32 = jnp.float32
VMEM_LIMIT = 48 * 1024 * 1024
WHOLE_VMEM = 63 * 1024 * 1024 + 512 * 1024


def rank_of(place, places):
    return place * 2 % places + place // (places // 2)


def place_of(rank, places):
    return rank // 2 + rank % 2 * (places // 2)


def reverse_bits(index, levels):
    return sum((index >> bit & 1) << levels - 1 - bit for bit in range(levels))


@functools.lru_cache(maxsize=None)
def tables(places, rows, width):
    levels = places.bit_length() - 1
    stride = 2 * places
    bins = stride * rows
    order = np.array([place_of(rank, places) for rank in range(places)])
    residues = np.array([2 * reverse_bits(place, levels) + parity for place in order for parity in range(2)])
    angle = 2.0 * np.pi * ((residues[:, None] * order[None, :]) % stride) / stride
    same = np.eye(width)
    first = np.concatenate([np.kron(np.cos(angle), same), np.kron(-np.sin(angle), same)])
    last = first.T / bins
    angle = 2.0 * np.pi * ((residues[:, None] * np.arange(rows)[None, :]) % bins) / bins
    twist = np.repeat(np.stack([np.cos(angle), np.sin(angle)]), width, axis=1)
    series = np.arange(rows)
    angle = 2.0 * np.pi * ((series[:, None] * series[None, :]) % rows) / rows
    dft = np.concatenate([np.cos(angle), np.sin(angle)])
    return (
        first.astype(jnp.bfloat16),
        last.astype(jnp.bfloat16),
        twist.astype(np.float32),
        dft.astype(jnp.bfloat16),
    )


def pair_rows(places):
    levels = places.bit_length() - 1

    def holder(residue):
        return rank_of(reverse_bits(residue // 2, levels), places), residue % 2

    mirrors = [None if residue % places == 0 else holder(2 * places - residue) for residue in range(places + 1)]
    return [holder(residue) for residue in range(places + 1)], mirrors


@functools.lru_cache(maxsize=None)
def folded_tables(places, rows, width):
    stride = 2 * places
    bins = stride * rows
    order = np.array([place_of(rank, places) for rank in range(places)])
    residues = np.arange(places + 1)
    angle = 2.0 * np.pi * ((residues[:, None] * order[None, :]) % stride) / stride
    same = np.eye(width)
    first = np.concatenate([np.kron(np.cos(angle), same), np.kron(-np.sin(angle), same)])
    last = first.T / bins
    angle = 2.0 * np.pi * ((residues[:, None] * np.arange(rows)[None, :]) % bins) / bins
    twist = np.stack([np.cos(angle), np.sin(angle)])
    block = rows // 4
    series = np.arange(block)
    angle = 2.0 * np.pi * ((np.arange(4)[:, None] * series[None, :]) % rows) / rows
    spin = np.stack([np.cos(angle), np.sin(angle)])
    angle = 2.0 * np.pi * ((series[:, None] * series[None, :]) % block) / block
    cos, sin = np.cos(angle), np.sin(angle)
    there = np.block([[cos, -sin], [sin, cos]])
    back = np.block([[cos, sin], [-sin, cos]])
    reverse = np.eye(block)[::-1]
    return (
        first.astype(jnp.bfloat16),
        last.astype(jnp.bfloat16),
        twist.astype(np.float32),
        spin.astype(np.float32),
        np.stack([there, back]).astype(jnp.bfloat16),
        reverse.astype(jnp.bfloat16),
    )


def hops(places):
    known, apart = [0], 1
    steps = [[0]]
    while apart < places:
        steps.append([apart ^ step for step in known])
        known = known + steps[-1]
        apart *= 2
    return steps


def prepare_kernel(
    features_ref,
    pre_ref,
    gain_ref,
    skip_ref,
    spectrum_ref,
    squares_ref,
    skipped_ref,
    packed_ref,
    features_in,
    pre_in,
    gain_in,
    skip_in,
    spectrum_in,
    squares_out,
    skipped_out,
    packed_out,
    in_sems,
    out_sems,
):
    blocks = [(part, parity) for part in range(2) for parity in range(2)]
    pairs = [(features_ref, features_in), (pre_ref, pre_in), (gain_ref, gain_in), (skip_ref, skip_in)]
    pairs += [(spectrum_ref.at[block], spectrum_in.at[block]) for block in blocks]
    arriving = [pltpu.make_async_copy(*pair, in_sems.at[slot]) for slot, pair in enumerate(pairs)]
    for copy in arriving:
        copy.start()
    leaving = []

    def leave(source, target):
        copy = pltpu.make_async_copy(source, target, out_sems.at[len(leaving)])
        copy.start()
        leaving.append(copy)

    def pack(slot, turned):
        if len(packed_ref.shape) == 4:
            places, width = packed_out.shape[1:3]
            for rank in range(places):
                begin = place_of(rank, places) * width
                packed_out[slot, rank] = turned[begin : begin + width]
            leave(packed_out.at[slot], packed_ref.at[:, slot])
        else:
            packed_out[slot] = turned
            leave(packed_out.at[slot], packed_ref.at[slot])

    for copy in arriving[:4]:
        copy.wait()
    features = features_in[...].astype(F32)
    scaled = (features * gain_in[...] * pre_in[...].astype(F32)).T
    pack(4, scaled.astype(BF16))
    skipped_out[...] = scaled * skip_in[...].reshape(-1, 1)
    leave(skipped_out, skipped_ref)
    turned = features.T
    squares_out[...] = jnp.sum(turned * turned, axis=0, keepdims=True)
    leave(squares_out, squares_ref)
    for slot, block in enumerate(blocks):
        arriving[4 + slot].wait()
        if len(packed_ref.shape) == 4:
            quarter = spectrum_in.shape[2] // 4
            rows = [spectrum_in[(*block, pl.ds(turn, quarter, stride=4), slice(None))] for turn in range(4)]
            pack(slot, jnp.concatenate([row.T for row in rows], axis=1).astype(BF16))
        else:
            pack(slot, spectrum_in[block].T.astype(BF16))
    for copy in leaving:
        copy.wait()


def scale_kernel(channels, *refs):
    square_refs, scale_ref = refs[:-1], refs[-1]
    total = square_refs[0][...]
    for square_ref in square_refs[1:]:
        total = total + square_ref[...]
    scale_ref[...] = lax.rsqrt(total / channels + EPS)


def matmul(left, right):
    return jnp.dot(left, right, preferred_element_type=F32)


def butterfly(values, direction):
    (real0, imag0), (real1, imag1), (real2, imag2), (real3, imag3) = values
    even, odd = (real0 + real2, imag0 + imag2), (real1 + real3, imag1 + imag3)
    even_gap, odd_gap = (real0 - real2, imag0 - imag2), (real1 - real3, imag1 - imag3)
    lower = (even_gap[0] + odd_gap[1], even_gap[1] - odd_gap[0])
    upper = (even_gap[0] - odd_gap[1], even_gap[1] + odd_gap[0])
    total, gap = (even[0] + odd[0], even[1] + odd[1]), (even[0] - odd[0], even[1] - odd[1])
    return [total, lower, gap, upper] if direction > 0 else [total, upper, gap, lower]


def folded_kernel(packed_ref, first_ref, last_ref, twist_ref, spin_ref, dft_ref, reverse_ref, *refs):
    scale_refs, (out_ref, scales, mirror, mixed, work, both) = refs[:-6], refs[-6:]
    wide, rows = out_ref.shape
    places, width = scales.shape[0], wide // scales.shape[0]
    half, block = first_ref.shape[0] // 2, rows // 4
    inner = half - 2 * width
    place = lax.axis_index("seq")
    for scale_ref, steps in zip(scale_refs, hops(places)):
        for at, step in enumerate(steps):
            scales[rank_of(place ^ step, places)] = scale_ref[pl.ds(at, 1), :]
    direct, mirrors = pair_rows(places)
    quarters = [pl.ds(turn * block, block) for turn in range(4)]
    signal = (packed_ref[:, 4].astype(F32) * scales[...]).astype(BF16).reshape(wide, rows)
    mixed[...] = matmul(first_ref[...], signal)
    for residue in range(places + 1):
        over, under = pl.ds(residue * width, width), pl.ds(half + residue * width, width)
        values = []
        for lanes in quarters:
            real, imag = mixed[over, lanes], mixed[under, lanes]
            cos, sin = twist_ref[0, pl.ds(residue, 1), lanes], twist_ref[1, pl.ds(residue, 1), lanes]
            values.append((real * cos + imag * sin, imag * cos - real * sin))
        for turn, (real, imag) in enumerate(butterfly(values, 1)):
            if turn > 0:
                cos, sin = spin_ref[0, pl.ds(turn, 1), :], spin_ref[1, pl.ds(turn, 1), :]
                real, imag = real * cos + imag * sin, imag * cos - real * sin
            at = pl.ds(turn * half + residue * width, width)
            work[at, pl.ds(0, block)] = real.astype(BF16)
            work[at, pl.ds(block, block)] = imag.astype(BF16)
    for row, holder in enumerate(mirrors[1:places]):
        for part in range(2):
            for turn in range(4):
                at = pl.ds((part * 4 + 3 - turn) * inner + row * width, width)
                mirror[at, :] = packed_ref[holder[0], 2 * part + holder[1], :, quarters[turn]]
    reversed_bins = matmul(mirror[...], reverse_ref[...])
    spectral = matmul(work[...], dft_ref[0])
    for turn in range(4):
        for residue, holder in enumerate(direct):
            at = turn * half + residue * width
            real, imag = spectral[at : at + width, :block], spectral[at : at + width, block:]
            response_real = packed_ref[holder[0], holder[1], :, quarters[turn]].astype(F32)
            response_imag = packed_ref[holder[0], 2 + holder[1], :, quarters[turn]].astype(F32)
            if mirrors[residue] is not None:
                begin = turn * inner + (residue - 1) * width
                response_real = response_real + reversed_bins[begin : begin + width]
                begin = begin + 4 * inner
                response_imag = response_imag - reversed_bins[begin : begin + width]
            work[pl.ds(at, width), pl.ds(0, block)] = (real * response_real - imag * response_imag).astype(BF16)
            work[pl.ds(at, width), pl.ds(block, block)] = (real * response_imag + imag * response_real).astype(BF16)
    restored = matmul(work[...], dft_ref[1])
    for residue in range(places + 1):
        values = []
        for turn in range(4):
            at = turn * half + residue * width
            real, imag = restored[at : at + width, :block], restored[at : at + width, block:]
            if turn > 0:
                cos, sin = spin_ref[0, pl.ds(turn, 1), :], spin_ref[1, pl.ds(turn, 1), :]
                real, imag = real * cos - imag * sin, imag * cos + real * sin
            values.append((real, imag))
        for lanes, (real, imag) in zip(quarters, butterfly(values, -1)):
            cos, sin = twist_ref[0, pl.ds(residue, 1), lanes], twist_ref[1, pl.ds(residue, 1), lanes]
            both[pl.ds(residue * width, width), lanes] = (real * cos - imag * sin).astype(BF16)
            both[pl.ds(half + residue * width, width), lanes] = (imag * cos + real * sin).astype(BF16)
    out_ref[...] = matmul(last_ref[...], both[...]).astype(BF16)


def convolve_kernel(packed_ref, first_ref, last_ref, twist_ref, dft_ref, scale_ref, out_ref, left, right):
    wide, rows = out_ref.shape
    half = 2 * wide
    signal = (packed_ref[4].astype(F32) * scale_ref[...]).astype(BF16)
    mixed = matmul(first_ref[...], signal)
    real, imag = mixed[:half], mixed[half:]
    cos_twist, sin_twist = twist_ref[0], twist_ref[1]
    turned_real = (real * cos_twist + imag * sin_twist).astype(BF16)
    turned_imag = (imag * cos_twist - real * sin_twist).astype(BF16)
    left[pl.ds(0, half), pl.ds(0, rows)] = turned_real
    left[pl.ds(0, half), pl.ds(rows, rows)] = turned_imag
    left[pl.ds(half, half), pl.ds(0, rows)] = turned_imag
    left[pl.ds(half, half), pl.ds(rows, rows)] = -turned_real
    mixed = matmul(left[...], dft_ref[...])
    real, imag = mixed[:half], mixed[half:]
    response_real = packed_ref[0:2].reshape(half, rows).astype(F32)
    response_imag = packed_ref[2:4].reshape(half, rows).astype(F32)
    product_real = (real * response_real - imag * response_imag).astype(BF16)
    product_imag = (real * response_imag + imag * response_real).astype(BF16)
    right[pl.ds(0, half), pl.ds(0, rows)] = product_real
    right[pl.ds(0, half), pl.ds(rows, rows)] = -product_imag
    right[pl.ds(half, half), pl.ds(0, rows)] = product_imag
    right[pl.ds(half, half), pl.ds(rows, rows)] = product_real
    mixed = matmul(right[...], dft_ref[...])
    real, imag = mixed[:half], mixed[half:]
    turned_real = (real * cos_twist - imag * sin_twist).astype(BF16)
    turned_imag = (imag * cos_twist + real * sin_twist).astype(BF16)
    both = jnp.concatenate([turned_real, turned_imag], axis=0)
    out_ref[...] = matmul(last_ref[...], both).astype(BF16)


def finish_kernel(conv_ref, skipped_ref, scale_ref, post_ref, out_ref):
    conv = conv_ref[...]
    if len(conv_ref.shape) == 3:
        places = conv_ref.shape[0]
        conv = jnp.concatenate([conv_ref[rank_of(place, places)] for place in range(places)])
    turned = conv.astype(F32) + skipped_ref[...] * scale_ref[...]
    out_ref[...] = (post_ref[...].astype(F32) * turned.T).astype(BF16)


def call(kernel, out_shape, flops, moved, *operands, limit=VMEM_LIMIT, **options):
    return pl.pallas_call(
        kernel,
        out_shape=out_shape,
        compiler_params=pltpu.CompilerParams(vmem_limit_bytes=limit),
        cost_estimate=pl.CostEstimate(flops=flops, bytes_accessed=moved, transcendentals=0),
        **options,
    )(*operands)


def exchange(value):
    places = lax.axis_size("seq")
    ranks = [[place_of(rank, places) for rank in range(places)]]
    return lax.all_to_all(value, "seq", split_axis=0, concat_axis=0, tiled=True, axis_index_groups=ranks)


def swap(value, axis, apart):
    return lax.ppermute(value, axis, [(place, place ^ apart) for place in range(lax.axis_size(axis))])


def local(features, pre_gate, post_gate, norm_gain, skip_weight, spectrum):
    rows, wide = features.shape
    places = lax.axis_size("seq")
    groups = lax.axis_size("chan")
    width = wide // places
    piled = width % 16 == 0
    cells = rows * wide
    shape = jax.ShapeDtypeStruct
    vmem, anywhere = pl.BlockSpec(memory_space=pltpu.VMEM), pl.BlockSpec(memory_space=pl.ANY)
    squares, skipped, packed = call(
        prepare_kernel,
        (
            shape((1, rows), F32),
            shape((wide, rows), F32),
            shape((places, 5, width, rows) if piled else (5, wide, rows), BF16),
        ),
        10 * cells,
        32 * cells,
        features,
        pre_gate,
        norm_gain[None, :],
        skip_weight[None, :],
        spectrum,
        limit=WHOLE_VMEM,
        in_specs=[anywhere] * 5,
        out_specs=(anywhere, anywhere, anywhere),
        scratch_shapes=[
            pltpu.VMEM(features.shape, BF16),
            pltpu.VMEM(pre_gate.shape, BF16),
            pltpu.VMEM((1, wide), F32),
            pltpu.VMEM((1, wide), F32),
            pltpu.VMEM(spectrum.shape, F32),
            pltpu.VMEM((1, rows), F32),
            pltpu.VMEM((wide, rows), F32),
            pltpu.VMEM((5, places, width, rows) if piled else (5, wide, rows), BF16),
            pltpu.SemaphoreType.DMA((8,)),
            pltpu.SemaphoreType.DMA((7,)),
        ],
    )
    if not piled:
        order = np.array([place_of(rank, places) for rank in range(places)])
        packed = packed.reshape(5, places, width, rows).transpose(1, 0, 2, 3)[order]
    gathered = exchange(packed)
    others = [swap(squares, "chan", apart) for apart in range(1, groups)]
    scale = call(
        functools.partial(scale_kernel, wide * groups), shape((1, rows), F32), 8 * rows, 32 * rows, squares, *others
    )
    if piled:
        scales, apart = [scale], 1
        while apart < places:
            known = jnp.concatenate(scales) if len(scales) > 1 else scale
            scales.append(swap(known, "seq", apart))
            apart *= 2
    else:
        scales = [jnp.repeat(lax.all_gather(scale, "seq", axis=0, tiled=True)[order], width, axis=0)]
        response = gathered[:, :4].reshape(places, 2, 2, width, rows).transpose(1, 0, 2, 3, 4)
        gathered = jnp.concatenate([response.reshape(4, wide, rows), gathered[:, 4].reshape(1, wide, rows)])
    if piled:
        constants = folded_tables(places, rows, width)
        half = constants[0].shape[0] // 2
        scratch = [
            pltpu.VMEM((places, 1, rows), F32),
            pltpu.VMEM((8 * (half - 2 * width), rows // 4), BF16),
            pltpu.VMEM((2 * half, rows), F32),
            pltpu.VMEM((4 * half, rows // 2), BF16),
            pltpu.VMEM((2 * half, rows), BF16),
        ]
    else:
        constants = tables(places, rows, width)
        scratch = [pltpu.VMEM((4 * wide, 2 * rows), BF16)] * 2
    conv = call(
        folded_kernel if piled else convolve_kernel,
        shape((wide, rows), BF16),
        20 * cells * rows,
        20 * cells,
        gathered,
        *constants,
        *scales,
        scratch_shapes=scratch,
    )
    conv = exchange(conv.reshape(places, width, rows))
    if not piled:
        conv = conv[np.array([rank_of(place, places) for place in range(places)])].reshape(wide, rows)
    return call(finish_kernel, shape((rows, wide), BF16), 10 * cells, 8 * cells, conv, skipped, scale, post_gate)


def solution(mesh):
    return jax.shard_map(
        local,
        mesh=mesh,
        in_specs=(
            P("seq", "chan"),
            P("seq", "chan"),
            P("seq", "chan"),
            P("chan"),
            P("chan"),
            P(None, "seq", None, "chan"),
        ),
        out_specs=P("seq", "chan"),
        check_vma=False,
    )
```

profile of v0, /device:TPU:0, one launch (start us, length us, event | category | flops | bytes accessed | tf_op | source)
XLA Modules:
  0.0 41.5 jit_solution(11645984752775379963)
XLA Ops:
  0.0 2.4 %shard_map.118 = (f32[1,512]{1,0:T(1,128)}, f32[128,512]{1,0:T(8,128)}, bf16[8,5,16,512]{3,2,1,0:T(8,128)(2,1)}) custom-call(bf16[512,128]{1,0:T(8,128)(2,1)} %features_ref.1, bf16[512,128]{1,0:T(8,128)(2,1)} %pre_ref.1, f32[1,128]{1,0:T(1,128)} %bitcast.4, f32[1,128]{1,0:T(1,128)} %bitcast.5, f32[2,2,512,128]{3,2,1,0:T(8,128)} %spectrum_ref.1), custom_call_target="tpu_custom_call" | custom-call | flops 655360 | bytes 2097152 | tf_op jit(solution)/shard_map/pallas_call | solution.py:299
  2.4 0.0 copy-start.2
  2.4 0.0 copy-start.3
  2.5 0.0 copy-start.4
  2.5 0.0 copy-start.5
  2.5 0.0 copy-start.6
  2.5 0.0 copy-start.8
  2.5 7.4 %all-to-all-start = ((bf16[8,5,16,512]{3,2,1,0:T(8,128)(2,1)}), bf16[8,5,16,512]{3,2,1,0:T(8,128)(2,1)S(1)}, u32[]{:S(2)}, u32[]{:S(2)}) async-start(bf16[8,5,16,512]{3,2,1,0:T(8,128)(2,1)} %get-tuple-element.8), calls=%async_computation | async-start | bytes 1310720 | tf_op jit(solution)/shard_map/all_to_all | solution.py:311
  9.9 0.0 copy-done.2
  9.9 0.7 %collective-permute-start.2 = (f32[1,512]{1,0:T(1,128)S(1)}, f32[1,512]{1,0:T(1,128)S(1)}, u32[]{:S(2)}, u32[]{:S(2)}) collective-permute-start(f32[1,512]{1,0:T(1,128)S(1)} %copy-done.2), channel_id=1, source_target_pairs={{0,3},{1,2},{2,1},{3,0},{4,7},{5,6},{6,5},{7,4},{8,11},{9,10},{10,... | collective-permute-start | bytes 6152 | tf_op jit(solution)/shard_map/ppermute | solution.py:315
  10.7 0.9 %collective-permute-start.1 = (f32[1,512]{1,0:T(1,128)S(1)}, f32[1,512]{1,0:T(1,128)S(1)}, u32[]{:S(2)}, u32[]{:S(2)}) collective-permute-start(f32[1,512]{1,0:T(1,128)S(1)} %copy-done.2), channel_id=1, source_target_pairs={{0,2},{1,3},{2,0},{3,1},{4,6},{5,7},{6,4},{7,5},{8,10},{9,11},{10,... | collective-permute-start | bytes 6152 | tf_op jit(solution)/shard_map/ppermute | solution.py:315
  11.6 0.3 collective-permute-start
  11.9 1.1 %collective-permute-done.2.refs_3_ = f32[1,512]{1,0:T(1,128)S(1)} collective-permute-done((f32[1,512]{1,0:T(1,128)S(1)}, f32[1,512]{1,0:T(1,128)S(1)}, u32[]{:S(2)}, u32[]{:S(2)}) %collective-permute-start.2) | collective-permute-done | bytes 2080 | tf_op jit(solution)/shard_map/ppermute | solution.py:315
  13.0 1.2 %collective-permute-done.1.refs_2_ = f32[1,512]{1,0:T(1,128)S(1)} collective-permute-done((f32[1,512]{1,0:T(1,128)S(1)}, f32[1,512]{1,0:T(1,128)S(1)}, u32[]{:S(2)}, u32[]{:S(2)}) %collective-permute-start.1) | collective-permute-done | bytes 2080 | tf_op jit(solution)/shard_map/ppermute | solution.py:315
  14.3 0.0 collective-permute-done.refs_1_
  14.3 1.8 %collective-permute-start.3 = (f32[1,512]{1,0:T(1,128)S(1)}, f32[1,512]{1,0:T(1,128)S(1)}, u32[]{:S(2)}, u32[]{:S(2)}) collective-permute-start(f32[1,512]{1,0:T(1,128)S(1)} %shard_map.119.refs_0_.scale_ref), channel_id=1, source_target_pairs={{0,4},{4,0},{8,12},{12,8},{16,20},{20,16},{24,28},{28,24},{1,5},{5... | collective-permute-start | bytes 6152 | tf_op jit(solution)/shard_map/ppermute | solution.py:315
  16.1 1.8 %collective-permute-done.3.refs_1_ = f32[1,512]{1,0:T(1,128)S(1)} collective-permute-done((f32[1,512]{1,0:T(1,128)S(1)}, f32[1,512]{1,0:T(1,128)S(1)}, u32[]{:S(2)}, u32[]{:S(2)}) %collective-permute-start.3) | collective-permute-done | bytes 2080 | tf_op jit(solution)/shard_map/ppermute | solution.py:315
  17.9 2.0 %collective-permute-start.4 = (f32[2,512]{1,0:T(2,128)S(1)}, f32[2,512]{1,0:T(2,128)S(1)}, u32[]{:S(2)}, u32[]{:S(2)}) collective-permute-start(f32[2,512]{1,0:T(2,128)S(1)} %pad_maximum_fusion.1), channel_id=1, source_target_pairs={{0,8},{4,12},{8,0},{12,4},{16,24},{20,28},{24,16},{28,20},{1,9},{5... | collective-permute-start | bytes 12296 | tf_op jit(solution)/shard_map/ppermute | solution.py:315
  19.9 1.8 %collective-permute-done.4.refs_2_ = f32[2,512]{1,0:T(2,128)S(1)} collective-permute-done((f32[2,512]{1,0:T(2,128)S(1)}, f32[2,512]{1,0:T(2,128)S(1)}, u32[]{:S(2)}, u32[]{:S(2)}) %collective-permute-start.4) | collective-permute-done | bytes 4128 | tf_op jit(solution)/shard_map/ppermute | solution.py:315
  21.7 3.7 %collective-permute-start.5 = (f32[4,512]{1,0:T(4,128)S(1)}, f32[4,512]{1,0:T(4,128)S(1)}, u32[]{:S(2)}, u32[]{:S(2)}) collective-permute-start(f32[4,512]{1,0:T(4,128)S(1)} %pad_maximum_fusion), channel_id=1, source_target_pairs={{0,16},{4,20},{8,24},{12,28},{16,0},{20,4},{24,8},{28,12},{1,17},{... | collective-permute-start | bytes 24584 | tf_op jit(solution)/shard_map/ppermute | solution.py:315
  25.4 2.1 %collective-permute-done.5.refs_3_ = f32[4,512]{1,0:T(4,128)S(1)} collective-permute-done((f32[4,512]{1,0:T(4,128)S(1)}, f32[4,512]{1,0:T(4,128)S(1)}, u32[]{:S(2)}, u32[]{:S(2)}) %collective-permute-start.5) | collective-permute-done | bytes 8224 | tf_op jit(solution)/shard_map/ppermute | solution.py:315
  27.5 0.0 all-to-all-done.packed_ref
  27.5 0.0 copy-done.3
  27.5 0.0 copy-done.4
  27.5 0.0 copy-done.5
  27.5 0.0 copy-done.6
  27.5 0.0 copy-start.1
  27.6 1.2 %shard_map.120 = bf16[128,512]{1,0:T(8,128)(2,1)S(1)} custom-call(bf16[8,5,16,512]{3,2,1,0:T(8,128)(2,1)S(1)} %all-to-all-done.packed_ref, bf16[288,128]{1,0:T(8,128)(2,1)S(1)} %copy-done.5, bf16[128,288]{1,0:T(8,128)(2,1)S(1)} %copy-done.4, f32[2,9,512]{2,1,0:T(8,128)S(1)} %copy-done.6, f32[2,4,128]{2,1,0:T(4,128)S(1)} %copy-done.8, ...), custom_call_target="tpu_custom_call" | custom-call | flops 671088640 | bytes 1310720 | tf_op jit(solution)/shard_map/pallas_call | solution.py:299
  28.8 0.0 copy-start
  28.8 11.9 %all_to_all.10.conv_ref = bf16[8,16,512]{2,1,0:T(8,128)(2,1)S(1)} all-to-all(bf16[8,16,512]{2,1,0:T(8,128)(2,1)S(1)} %bitcast.3), channel_id=1, replica_groups={{0,16,4,20,8,24,12,28},{1,17,5,21,9,25,13,29},{2,18,6,22,10,26,14,30},{..., dimensions={0} | all-to-all | bytes 262144 | tf_op jit(solution)/shard_map/all_to_all | solution.py:311
  40.7 0.0 copy-done
  40.7 0.8 %shard_map.121 = bf16[512,128]{1,0:T(8,128)(2,1)} custom-call(bf16[8,16,512]{2,1,0:T(8,128)(2,1)S(1)} %all_to_all.10.conv_ref, f32[128,512]{1,0:T(8,128)S(1)} %copy-done, f32[1,512]{1,0:T(1,128)S(1)} %shard_map.119.refs_0_.scale_ref, bf16[512,128]{1,0:T(8,128)(2,1)S(1)} %copy-done.1), custom_call_target="tpu_custom_call" | custom-call | flops 655360 | bytes 524288 | tf_op jit(solution)/shard_map/pallas_call | solution.py:299
  (7 shorter events, 0.0 us)
Async XLA Ops:
  2.4 7.5 %copy-start.2 = (f32[1,512]{1,0:T(1,128)S(1)}, f32[1,512]{1,0:T(1,128)}, u32[]{:S(2)}) copy-start(f32[1,512]{1,0:T(1,128)} %get-tuple-element.9.refs_0_) | copy-start | bytes 6148
  2.4 25.1 %copy-start.3 = (bf16[2,256,256]{2,1,0:T(8,128)(2,1)S(1)}, bf16[2,256,256]{2,1,0:T(8,128)(2,1)}, u32[]{:S(2)}) copy-start(bf16[2,256,256]{2,1,0:T(8,128)(2,1)} %constant.16.clone.dft_ref) | copy-start | bytes 786436
  2.5 25.0 %copy-start.4 = (bf16[128,288]{1,0:T(8,128)(2,1)S(1)}, bf16[128,288]{1,0:T(8,128)(2,1)}, u32[]{:S(2)}) copy-start(bf16[128,288]{1,0:T(8,128)(2,1)} %constant.13.clone.last_ref) | copy-start | bytes 221188
  2.5 25.0 %copy-start.5 = (bf16[288,128]{1,0:T(8,128)(2,1)S(1)}, bf16[288,128]{1,0:T(8,128)(2,1)}, u32[]{:S(2)}) copy-start(bf16[288,128]{1,0:T(8,128)(2,1)} %constant.12.clone.first_ref) | copy-start | bytes 221188
  2.5 25.0 %copy-start.6 = (f32[2,9,512]{2,1,0:T(8,128)S(1)}, f32[2,9,512]{2,1,0:T(8,128)}, u32[]{:S(2)}) copy-start(f32[2,9,512]{2,1,0:T(8,128)} %constant.14.clone.twist_ref) | copy-start | bytes 110596
  2.5 25.0 %copy-start.8 = (f32[2,4,128]{2,1,0:T(4,128)S(1)}, f32[2,4,128]{2,1,0:T(4,128)}, u32[]{:S(2)}) copy-start(f32[2,4,128]{2,1,0:T(4,128)} %constant.15.clone.spin_ref) | copy-start | bytes 12292
  2.5 25.0 %all-to-all-start = ((bf16[8,5,16,512]{3,2,1,0:T(8,128)(2,1)}), bf16[8,5,16,512]{3,2,1,0:T(8,128)(2,1)S(1)}, u32[]{:S(2)}, u32[]{:S(2)}) async-start(bf16[8,5,16,512]{3,2,1,0:T(8,128)(2,1)} %get-tuple-element.8), calls=%async_computation | async-start | bytes 1310720 | tf_op jit(solution)/shard_map/all_to_all | solution.py:311
  9.9 17.6 %copy-start.7 = (bf16[128,128]{1,0:T(8,128)(2,1)S(1)}, bf16[128,128]{1,0:T(8,128)(2,1)}, u32[]{:S(2)}) copy-start(bf16[128,128]{1,0:T(8,128)(2,1)} %constant.17.clone.reverse_ref) | copy-start | bytes 98308
  9.9 3.1 %collective-permute-start.2 = (f32[1,512]{1,0:T(1,128)S(1)}, f32[1,512]{1,0:T(1,128)S(1)}, u32[]{:S(2)}, u32[]{:S(2)}) collective-permute-start(f32[1,512]{1,0:T(1,128)S(1)} %copy-done.2), channel_id=1, source_target_pairs={{0,3},{1,2},{2,1},{3,0},{4,7},{5,6},{6,5},{7,4},{8,11},{9,10},{10,... | collective-permute-start | bytes 6152 | tf_op jit(solution)/shard_map/ppermute | solution.py:315
  10.7 3.6 %collective-permute-start.1 = (f32[1,512]{1,0:T(1,128)S(1)}, f32[1,512]{1,0:T(1,128)S(1)}, u32[]{:S(2)}, u32[]{:S(2)}) collective-permute-start(f32[1,512]{1,0:T(1,128)S(1)} %copy-done.2), channel_id=1, source_target_pairs={{0,2},{1,3},{2,0},{3,1},{4,6},{5,7},{6,4},{7,5},{8,10},{9,11},{10,... | collective-permute-start | bytes 6152 | tf_op jit(solution)/shard_map/ppermute | solution.py:315
  11.6 2.7 %collective-permute-start = (f32[1,512]{1,0:T(1,128)S(1)}, f32[1,512]{1,0:T(1,128)S(1)}, u32[]{:S(2)}, u32[]{:S(2)}) collective-permute-start(f32[1,512]{1,0:T(1,128)S(1)} %copy-done.2), channel_id=1, source_target_pairs={{0,1},{1,0},{2,3},{3,2},{4,5},{5,4},{6,7},{7,6},{8,9},{9,8},{10,11... | collective-permute-start | bytes 6152 | tf_op jit(solution)/shard_map/ppermute | solution.py:315
  14.3 3.7 %collective-permute-start.3 = (f32[1,512]{1,0:T(1,128)S(1)}, f32[1,512]{1,0:T(1,128)S(1)}, u32[]{:S(2)}, u32[]{:S(2)}) collective-permute-start(f32[1,512]{1,0:T(1,128)S(1)} %shard_map.119.refs_0_.scale_ref), channel_id=1, source_target_pairs={{0,4},{4,0},{8,12},{12,8},{16,20},{20,16},{24,28},{28,24},{1,5},{5... | collective-permute-start | bytes 6152 | tf_op jit(solution)/shard_map/ppermute | solution.py:315
  17.9 3.8 %collective-permute-start.4 = (f32[2,512]{1,0:T(2,128)S(1)}, f32[2,512]{1,0:T(2,128)S(1)}, u32[]{:S(2)}, u32[]{:S(2)}) collective-permute-start(f32[2,512]{1,0:T(2,128)S(1)} %pad_maximum_fusion.1), channel_id=1, source_target_pairs={{0,8},{4,12},{8,0},{12,4},{16,24},{20,28},{24,16},{28,20},{1,9},{5... | collective-permute-start | bytes 12296 | tf_op jit(solution)/shard_map/ppermute | solution.py:315
  21.7 5.8 %collective-permute-start.5 = (f32[4,512]{1,0:T(4,128)S(1)}, f32[4,512]{1,0:T(4,128)S(1)}, u32[]{:S(2)}, u32[]{:S(2)}) collective-permute-start(f32[4,512]{1,0:T(4,128)S(1)} %pad_maximum_fusion), channel_id=1, source_target_pairs={{0,16},{4,20},{8,24},{12,28},{16,0},{20,4},{24,8},{28,12},{1,17},{... | collective-permute-start | bytes 24584 | tf_op jit(solution)/shard_map/ppermute | solution.py:315
  27.5 13.2 %copy-start.1 = (bf16[512,128]{1,0:T(8,128)(2,1)S(1)}, bf16[512,128]{1,0:T(8,128)(2,1)}, u32[]{:S(2)}) copy-start(bf16[512,128]{1,0:T(8,128)(2,1)} %post_ref.1) | copy-start | bytes 393220
  28.8 11.9 %copy-start = (f32[128,512]{1,0:T(8,128)S(1)}, f32[128,512]{1,0:T(8,128)}, u32[]{:S(2)}) copy-start(f32[128,512]{1,0:T(8,128)} %get-tuple-element.10.skipped_ref) | copy-start | bytes 786436
where the time goes:
time: 41.8 us; the launch traced here: 41.5 us
  starting transfers between devices  16.8 us (40%)
  blocking collectives  11.9 us (28%)
  waiting for transfers between devices  8.09 us (19%)
  Pallas kernels  4.46 us (11%)
    all_to_all x1, blocking collectives, exchange(): lax.all_to_all(value, 'seq', split_axis=0, concat_axis=0, tiled=True, axi...  11.9 us
    ppermute x6, starting transfers between devices, swap(): lax.ppermute(value, axis, [(place, place ^ apart) for place in range(lax....  9.41 us
    ppermute x6, waiting for transfers between devices, swap(): lax.ppermute(value, axis, [(place, place ^ apart) for place in range(lax....  8.09 us
    all_to_all x1, starting transfers between devices, exchange(): lax.all_to_all(value, 'seq', split_axis=0, concat_axis=0, tiled=True, axi...  7.42 us
    pallas_call x4, Pallas kernels, call(): pl.pallas_call(kernel, out_shape=out_shape, compiler_params=pltpu.Compile...  4.46 us
  transfers between devices with their start and end apart: 7, of which 5 were waited for; matrix products, arithmetic and copies ran while one was open for 0% of the time, Pallas kernels for 0%

commit v1 on v0

--- a/solution.py
+++ b/solution.py
@@ -15,14 +15,6 @@
 WHOLE_VMEM = 63 * 1024 * 1024 + 512 * 1024
 
 
-def rank_of(place, places):
-    return place * 2 % places + place // (places // 2)
-
-
-def place_of(rank, places):
-    return rank // 2 + rank % 2 * (places // 2)
-
-
 def reverse_bits(index, levels):
     return sum((index >> bit & 1) << levels - 1 - bit for bit in range(levels))
 
@@ -32,9 +24,8 @@
     levels = places.bit_length() - 1
     stride = 2 * places
     bins = stride * rows
-    order = np.array([place_of(rank, places) for rank in range(places)])
-    residues = np.array([2 * reverse_bits(place, levels) + parity for place in order for parity in range(2)])
-    angle = 2.0 * np.pi * ((residues[:, None] * order[None, :]) % stride) / stride
+    residues = np.array([2 * reverse_bits(place, levels) + parity for place in range(places) for parity in range(2)])
+    angle = 2.0 * np.pi * ((residues[:, None] * np.arange(places)[None, :]) % stride) / stride
     same = np.eye(width)
     first = np.concatenate([np.kron(np.cos(angle), same), np.kron(-np.sin(angle), same)])
     last = first.T / bins
@@ -55,7 +46,7 @@
     levels = places.bit_length() - 1
 
     def holder(residue):
-        return rank_of(reverse_bits(residue // 2, levels), places), residue % 2
+        return reverse_bits(residue // 2, levels), residue % 2
 
     mirrors = [None if residue % places == 0 else holder(2 * places - residue) for residue in range(places + 1)]
     return [holder(residue) for residue in range(places + 1)], mirrors
@@ -65,9 +56,8 @@
 def folded_tables(places, rows, width):
     stride = 2 * places
     bins = stride * rows
-    order = np.array([place_of(rank, places) for rank in range(places)])
     residues = np.arange(places + 1)
-    angle = 2.0 * np.pi * ((residues[:, None] * order[None, :]) % stride) / stride
+    angle = 2.0 * np.pi * ((residues[:, None] * np.arange(places)[None, :]) % stride) / stride
     same = np.eye(width)
     first = np.concatenate([np.kron(np.cos(angle), same), np.kron(-np.sin(angle), same)])
     last = first.T / bins
@@ -137,10 +127,7 @@
 
     def pack(slot, turned):
         if len(packed_ref.shape) == 4:
-            places, width = packed_out.shape[1:3]
-            for rank in range(places):
-                begin = place_of(rank, places) * width
-                packed_out[slot, rank] = turned[begin : begin + width]
+            packed_out[slot] = turned.reshape(packed_out.shape[1:])
             leave(packed_out.at[slot], packed_ref.at[:, slot])
         else:
             packed_out[slot] = turned
@@ -199,7 +186,7 @@
     place = lax.axis_index("seq")
     for scale_ref, steps in zip(scale_refs, hops(places)):
         for at, step in enumerate(steps):
-            scales[rank_of(place ^ step, places)] = scale_ref[pl.ds(at, 1), :]
+            scales[place ^ step] = scale_ref[pl.ds(at, 1), :]
     direct, mirrors = pair_rows(places)
     quarters = [pl.ds(turn * block, block) for turn in range(4)]
     signal = (packed_ref[:, 4].astype(F32) * scales[...]).astype(BF16).reshape(wide, rows)
@@ -287,11 +274,7 @@
 
 
 def finish_kernel(conv_ref, skipped_ref, scale_ref, post_ref, out_ref):
-    conv = conv_ref[...]
-    if len(conv_ref.shape) == 3:
-        places = conv_ref.shape[0]
-        conv = jnp.concatenate([conv_ref[rank_of(place, places)] for place in range(places)])
-    turned = conv.astype(F32) + skipped_ref[...] * scale_ref[...]
+    turned = conv_ref[...].astype(F32) + skipped_ref[...] * scale_ref[...]
     out_ref[...] = (post_ref[...].astype(F32) * turned.T).astype(BF16)
 
 
@@ -306,9 +289,7 @@
 
 
 def exchange(value):
-    places = lax.axis_size("seq")
-    ranks = [[place_of(rank, places) for rank in range(places)]]
-    return lax.all_to_all(value, "seq", split_axis=0, concat_axis=0, tiled=True, axis_index_groups=ranks)
+    return lax.all_to_all(value, "seq", split_axis=0, concat_axis=0, tiled=True)
 
 
 def swap(value, axis, apart):
@@ -355,8 +336,7 @@
         ],
     )
     if not piled:
-        order = np.array([place_of(rank, places) for rank in range(places)])
-        packed = packed.reshape(5, places, width, rows).transpose(1, 0, 2, 3)[order]
+        packed = packed.reshape(5, places, width, rows).transpose(1, 0, 2, 3)
     gathered = exchange(packed)
     others = [swap(squares, "chan", apart) for apart in range(1, groups)]
     scale = call(
@@ -369,7 +349,7 @@
             scales.append(swap(known, "seq", apart))
             apart *= 2
     else:
-        scales = [jnp.repeat(lax.all_gather(scale, "seq", axis=0, tiled=True)[order], width, axis=0)]
+        scales = [jnp.repeat(lax.all_gather(scale, "seq", axis=0, tiled=True), width, axis=0)]
         response = gathered[:, :4].reshape(places, 2, 2, width, rows).transpose(1, 0, 2, 3, 4)
         gathered = jnp.concatenate([response.reshape(4, wide, rows), gathered[:, 4].reshape(1, wide, rows)])
     if piled:
@@ -395,9 +375,7 @@
         *scales,
         scratch_shapes=scratch,
     )
-    conv = exchange(conv.reshape(places, width, rows))
-    if not piled:
-        conv = conv[np.array([rank_of(place, places) for place in range(places)])].reshape(wide, rows)
+    conv = exchange(conv.reshape(places, width, rows)).reshape(wide, rows)
     return call(finish_kernel, shape((rows, wide), BF16), 10 * cells, 8 * cells, conv, skipped, scale, post_gate)
 
 

time: 41.8 us -> 41.8 us (level)
  no operation moved by 1% of the time
where the time goes in v1:
time: 41.8 us; the launch traced here: 41.5 us
  starting transfers between devices  16.7 us (40%)
  blocking collectives  11.9 us (28%)
  waiting for transfers between devices  8.35 us (20%)
  Pallas kernels  4.4 us (11%)
    all_to_all x1, blocking collectives, exchange(): return lax.all_to_all(value, 'seq', split_axis=0, concat_axis=0, tiled=True)  11.9 us
    ppermute x6, starting transfers between devices, swap(): lax.ppermute(value, axis, [(place, place ^ apart) for place in range(lax....  9.24 us
    ppermute x6, waiting for transfers between devices, swap(): lax.ppermute(value, axis, [(place, place ^ apart) for place in range(lax....  8.35 us
    all_to_all x1, starting transfers between devices, exchange(): return lax.all_to_all(value, 'seq', split_axis=0, concat_axis=0, tiled=True)  7.42 us
    pallas_call x4, Pallas kernels, call(): pl.pallas_call(kernel, out_shape=out_shape, compiler_params=pltpu.Compile...  4.4 us
  transfers between devices with their start and end apart: 7, of which 5 were waited for; matrix products, arithmetic and copies ran while one was open for 0% of the time, Pallas kernels for 0%

profile of v1, /device:TPU:0, one launch (start us, length us, event | category | flops | bytes accessed | tf_op | source)
XLA Modules:
  0.0 41.5 jit_solution(11188232420450906974)
XLA Ops:
  0.0 2.4 %shard_map.118 = (f32[1,512]{1,0:T(1,128)}, f32[128,512]{1,0:T(8,128)}, bf16[8,5,16,512]{3,2,1,0:T(8,128)(2,1)}) custom-call(bf16[512,128]{1,0:T(8,128)(2,1)} %features_ref.1, bf16[512,128]{1,0:T(8,128)(2,1)} %pre_ref.1, f32[1,128]{1,0:T(1,128)} %bitcast.6, f32[1,128]{1,0:T(1,128)} %bitcast.7, f32[2,2,512,128]{3,2,1,0:T(8,128)} %spectrum_ref.1), custom_call_target="tpu_custom_call" | custom-call | flops 655360 | bytes 2097152 | tf_op jit(solution)/shard_map/pallas_call | solution.py:282
  2.4 0.0 copy-start.2
  2.4 0.0 copy-start.3
  2.5 0.0 copy-start.4
  2.5 0.0 copy-start.5
  2.5 0.0 copy-start.6
  2.5 0.0 copy-start.8
  2.5 7.4 %all-to-all-start = ((bf16[8,5,16,512]{3,2,1,0:T(8,128)(2,1)}), bf16[8,5,16,512]{3,2,1,0:T(8,128)(2,1)S(1)}, u32[]{:S(2)}, u32[]{:S(2)}) async-start(bf16[8,5,16,512]{3,2,1,0:T(8,128)(2,1)} %get-tuple-element.8), calls=%async_computation | async-start | bytes 1310720 | tf_op jit(solution)/shard_map/all_to_all | solution.py:292
  9.9 0.0 copy-done.2
  9.9 0.7 %collective-permute-start.2 = (f32[1,512]{1,0:T(1,128)S(1)}, f32[1,512]{1,0:T(1,128)S(1)}, u32[]{:S(2)}, u32[]{:S(2)}) collective-permute-start(f32[1,512]{1,0:T(1,128)S(1)} %copy-done.2), channel_id=1, source_target_pairs={{0,3},{1,2},{2,1},{3,0},{4,7},{5,6},{6,5},{7,4},{8,11},{9,10},{10,... | collective-permute-start | bytes 6152 | tf_op jit(solution)/shard_map/ppermute | solution.py:296
  10.7 0.9 %collective-permute-start.1 = (f32[1,512]{1,0:T(1,128)S(1)}, f32[1,512]{1,0:T(1,128)S(1)}, u32[]{:S(2)}, u32[]{:S(2)}) collective-permute-start(f32[1,512]{1,0:T(1,128)S(1)} %copy-done.2), channel_id=1, source_target_pairs={{0,2},{1,3},{2,0},{3,1},{4,6},{5,7},{6,4},{7,5},{8,10},{9,11},{10,... | collective-permute-start | bytes 6152 | tf_op jit(solution)/shard_map/ppermute | solution.py:296
  11.6 0.3 collective-permute-start
  11.9 1.1 %collective-permute-done.2.refs_3_ = f32[1,512]{1,0:T(1,128)S(1)} collective-permute-done((f32[1,512]{1,0:T(1,128)S(1)}, f32[1,512]{1,0:T(1,128)S(1)}, u32[]{:S(2)}, u32[]{:S(2)}) %collective-permute-start.2) | collective-permute-done | bytes 2080 | tf_op jit(solution)/shard_map/ppermute | solution.py:296
  13.0 1.2 %collective-permute-done.1.refs_2_ = f32[1,512]{1,0:T(1,128)S(1)} collective-permute-done((f32[1,512]{1,0:T(1,128)S(1)}, f32[1,512]{1,0:T(1,128)S(1)}, u32[]{:S(2)}, u32[]{:S(2)}) %collective-permute-start.1) | collective-permute-done | bytes 2080 | tf_op jit(solution)/shard_map/ppermute | solution.py:296
  14.3 0.0 collective-permute-done.refs_1_
  14.3 1.8 %collective-permute-start.3 = (f32[1,512]{1,0:T(1,128)S(1)}, f32[1,512]{1,0:T(1,128)S(1)}, u32[]{:S(2)}, u32[]{:S(2)}) collective-permute-start(f32[1,512]{1,0:T(1,128)S(1)} %shard_map.119.refs_0_.scale_ref), channel_id=1, source_target_pairs={{0,4},{4,0},{8,12},{12,8},{16,20},{20,16},{24,28},{28,24},{1,5},{5... | collective-permute-start | bytes 6152 | tf_op jit(solution)/shard_map/ppermute | solution.py:296
  16.1 1.9 %collective-permute-done.3.refs_1_ = f32[1,512]{1,0:T(1,128)S(1)} collective-permute-done((f32[1,512]{1,0:T(1,128)S(1)}, f32[1,512]{1,0:T(1,128)S(1)}, u32[]{:S(2)}, u32[]{:S(2)}) %collective-permute-start.3) | collective-permute-done | bytes 2080 | tf_op jit(solution)/shard_map/ppermute | solution.py:296
  18.0 1.8 %collective-permute-start.4 = (f32[2,512]{1,0:T(2,128)S(1)}, f32[2,512]{1,0:T(2,128)S(1)}, u32[]{:S(2)}, u32[]{:S(2)}) collective-permute-start(f32[2,512]{1,0:T(2,128)S(1)} %pad_maximum_fusion.1), channel_id=1, source_target_pairs={{0,8},{4,12},{8,0},{12,4},{16,24},{20,28},{24,16},{28,20},{1,9},{5... | collective-permute-start | bytes 12296 | tf_op jit(solution)/shard_map/ppermute | solution.py:296
  19.8 1.9 %collective-permute-done.4.refs_2_ = f32[2,512]{1,0:T(2,128)S(1)} collective-permute-done((f32[2,512]{1,0:T(2,128)S(1)}, f32[2,512]{1,0:T(2,128)S(1)}, u32[]{:S(2)}, u32[]{:S(2)}) %collective-permute-start.4) | collective-permute-done | bytes 4128 | tf_op jit(solution)/shard_map/ppermute | solution.py:296
  21.7 3.7 %collective-permute-start.5 = (f32[4,512]{1,0:T(4,128)S(1)}, f32[4,512]{1,0:T(4,128)S(1)}, u32[]{:S(2)}, u32[]{:S(2)}) collective-permute-start(f32[4,512]{1,0:T(4,128)S(1)} %pad_maximum_fusion), channel_id=1, source_target_pairs={{0,16},{4,20},{8,24},{12,28},{16,0},{20,4},{24,8},{28,12},{1,17},{... | collective-permute-start | bytes 24584 | tf_op jit(solution)/shard_map/ppermute | solution.py:296
  25.4 2.2 %collective-permute-done.5.refs_3_ = f32[4,512]{1,0:T(4,128)S(1)} collective-permute-done((f32[4,512]{1,0:T(4,128)S(1)}, f32[4,512]{1,0:T(4,128)S(1)}, u32[]{:S(2)}, u32[]{:S(2)}) %collective-permute-start.5) | collective-permute-done | bytes 8224 | tf_op jit(solution)/shard_map/ppermute | solution.py:296
  27.6 0.0 all-to-all-done.packed_ref
  27.6 0.0 copy-done.3
  27.6 0.0 copy-done.4
  27.6 0.0 copy-done.5
  27.6 0.0 copy-done.6
  27.6 0.0 copy-done.8
  27.6 0.0 copy-done.7
  27.6 0.0 copy-start.1
  27.6 1.2 %shard_map.120 = bf16[128,512]{1,0:T(8,128)(2,1)S(1)} custom-call(bf16[8,5,16,512]{3,2,1,0:T(8,128)(2,1)S(1)} %all-to-all-done.packed_ref, bf16[288,128]{1,0:T(8,128)(2,1)S(1)} %copy-done.5, bf16[128,288]{1,0:T(8,128)(2,1)S(1)} %copy-done.4, f32[2,9,512]{2,1,0:T(8,128)S(1)} %copy-done.6, f32[2,4,128]{2,1,0:T(4,128)S(1)} %copy-done.8, ...), custom_call_target="tpu_custom_call" | custom-call | flops 671088640 | bytes 1310720 | tf_op jit(solution)/shard_map/pallas_call | solution.py:282
  28.8 11.9 %all_to_all.10 = bf16[8,16,512]{2,1,0:T(8,128)(2,1)S(1)} all-to-all(bf16[8,16,512]{2,1,0:T(8,128)(2,1)S(1)} %bitcast.5), channel_id=1, replica_groups=mesh['seq'=8,'chan'=4] {'seq'}, dimensions={0} | all-to-all | bytes 262144 | tf_op jit(solution)/shard_map/all_to_all | solution.py:292
  40.7 0.8 %shard_map.121 = bf16[512,128]{1,0:T(8,128)(2,1)} custom-call(bf16[128,512]{1,0:T(8,128)(2,1)S(1)} %bitcast.4, f32[128,512]{1,0:T(8,128)S(1)} %copy-done, f32[1,512]{1,0:T(1,128)S(1)} %shard_map.119.refs_0_.scale_ref, bf16[512,128]{1,0:T(8,128)(2,1)S(1)} %copy-done.1), custom_call_target="tpu_custom_call" | custom-call | flops 655360 | bytes 524288 | tf_op jit(solution)/shard_map/pallas_call | solution.py:282
  (7 shorter events, 0.0 us)
Async XLA Ops:
  2.4 7.5 %copy-start.2 = (f32[1,512]{1,0:T(1,128)S(1)}, f32[1,512]{1,0:T(1,128)}, u32[]{:S(2)}) copy-start(f32[1,512]{1,0:T(1,128)} %get-tuple-element.9.refs_0_) | copy-start | bytes 6148
  2.4 25.1 %copy-start.3 = (bf16[2,256,256]{2,1,0:T(8,128)(2,1)S(1)}, bf16[2,256,256]{2,1,0:T(8,128)(2,1)}, u32[]{:S(2)}) copy-start(bf16[2,256,256]{2,1,0:T(8,128)(2,1)} %constant.16.clone.dft_ref) | copy-start | bytes 786436
  2.5 25.1 %copy-start.4 = (bf16[128,288]{1,0:T(8,128)(2,1)S(1)}, bf16[128,288]{1,0:T(8,128)(2,1)}, u32[]{:S(2)}) copy-start(bf16[128,288]{1,0:T(8,128)(2,1)} %constant.13.clone.last_ref) | copy-start | bytes 221188
  2.5 25.1 %copy-start.5 = (bf16[288,128]{1,0:T(8,128)(2,1)S(1)}, bf16[288,128]{1,0:T(8,128)(2,1)}, u32[]{:S(2)}) copy-start(bf16[288,128]{1,0:T(8,128)(2,1)} %constant.12.clone.first_ref) | copy-start | bytes 221188
  2.5 25.1 %copy-start.6 = (f32[2,9,512]{2,1,0:T(8,128)S(1)}, f32[2,9,512]{2,1,0:T(8,128)}, u32[]{:S(2)}) copy-start(f32[2,9,512]{2,1,0:T(8,128)} %constant.14.clone.twist_ref) | copy-start | bytes 110596
  2.5 25.1 %copy-start.8 = (f32[2,4,128]{2,1,0:T(4,128)S(1)}, f32[2,4,128]{2,1,0:T(4,128)}, u32[]{:S(2)}) copy-start(f32[2,4,128]{2,1,0:T(4,128)} %constant.15.clone.spin_ref) | copy-start | bytes 12292
  2.5 25.1 %all-to-all-start = ((bf16[8,5,16,512]{3,2,1,0:T(8,128)(2,1)}), bf16[8,5,16,512]{3,2,1,0:T(8,128)(2,1)S(1)}, u32[]{:S(2)}, u32[]{:S(2)}) async-start(bf16[8,5,16,512]{3,2,1,0:T(8,128)(2,1)} %get-tuple-element.8), calls=%async_computation | async-start | bytes 1310720 | tf_op jit(solution)/shard_map/all_to_all | solution.py:292
  9.9 17.7 %copy-start.7 = (bf16[128,128]{1,0:T(8,128)(2,1)S(1)}, bf16[128,128]{1,0:T(8,128)(2,1)}, u32[]{:S(2)}) copy-start(bf16[128,128]{1,0:T(8,128)(2,1)} %constant.17.clone.reverse_ref) | copy-start | bytes 98308
  9.9 3.1 %collective-permute-start.2 = (f32[1,512]{1,0:T(1,128)S(1)}, f32[1,512]{1,0:T(1,128)S(1)}, u32[]{:S(2)}, u32[]{:S(2)}) collective-permute-start(f32[1,512]{1,0:T(1,128)S(1)} %copy-done.2), channel_id=1, source_target_pairs={{0,3},{1,2},{2,1},{3,0},{4,7},{5,6},{6,5},{7,4},{8,11},{9,10},{10,... | collective-permute-start | bytes 6152 | tf_op jit(solution)/shard_map/ppermute | solution.py:296
  10.7 3.6 %collective-permute-start.1 = (f32[1,512]{1,0:T(1,128)S(1)}, f32[1,512]{1,0:T(1,128)S(1)}, u32[]{:S(2)}, u32[]{:S(2)}) collective-permute-start(f32[1,512]{1,0:T(1,128)S(1)} %copy-done.2), channel_id=1, source_target_pairs={{0,2},{1,3},{2,0},{3,1},{4,6},{5,7},{6,4},{7,5},{8,10},{9,11},{10,... | collective-permute-start | bytes 6152 | tf_op jit(solution)/shard_map/ppermute | solution.py:296
  11.6 2.7 %collective-permute-start = (f32[1,512]{1,0:T(1,128)S(1)}, f32[1,512]{1,0:T(1,128)S(1)}, u32[]{:S(2)}, u32[]{:S(2)}) collective-permute-start(f32[1,512]{1,0:T(1,128)S(1)} %copy-done.2), channel_id=1, source_target_pairs={{0,1},{1,0},{2,3},{3,2},{4,5},{5,4},{6,7},{7,6},{8,9},{9,8},{10,11... | collective-permute-start | bytes 6152 | tf_op jit(solution)/shard_map/ppermute | solution.py:296
  14.3 3.7 %collective-permute-start.3 = (f32[1,512]{1,0:T(1,128)S(1)}, f32[1,512]{1,0:T(1,128)S(1)}, u32[]{:S(2)}, u32[]{:S(2)}) collective-permute-start(f32[1,512]{1,0:T(1,128)S(1)} %shard_map.119.refs_0_.scale_ref), channel_id=1, source_target_pairs={{0,4},{4,0},{8,12},{12,8},{16,20},{20,16},{24,28},{28,24},{1,5},{5... | collective-permute-start | bytes 6152 | tf_op jit(solution)/shard_map/ppermute | solution.py:296
  18.0 3.7 %collective-permute-start.4 = (f32[2,512]{1,0:T(2,128)S(1)}, f32[2,512]{1,0:T(2,128)S(1)}, u32[]{:S(2)}, u32[]{:S(2)}) collective-permute-start(f32[2,512]{1,0:T(2,128)S(1)} %pad_maximum_fusion.1), channel_id=1, source_target_pairs={{0,8},{4,12},{8,0},{12,4},{16,24},{20,28},{24,16},{28,20},{1,9},{5... | collective-permute-start | bytes 12296 | tf_op jit(solution)/shard_map/ppermute | solution.py:296
  21.7 5.9 %collective-permute-start.5 = (f32[4,512]{1,0:T(4,128)S(1)}, f32[4,512]{1,0:T(4,128)S(1)}, u32[]{:S(2)}, u32[]{:S(2)}) collective-permute-start(f32[4,512]{1,0:T(4,128)S(1)} %pad_maximum_fusion), channel_id=1, source_target_pairs={{0,16},{4,20},{8,24},{12,28},{16,0},{20,4},{24,8},{28,12},{1,17},{... | collective-permute-start | bytes 24584 | tf_op jit(solution)/shard_map/ppermute | solution.py:296
  27.6 13.1 %copy-start.1 = (bf16[512,128]{1,0:T(8,128)(2,1)S(1)}, bf16[512,128]{1,0:T(8,128)(2,1)}, u32[]{:S(2)}) copy-start(bf16[512,128]{1,0:T(8,128)(2,1)} %post_ref.1) | copy-start | bytes 393220
  28.8 11.9 %copy-start = (f32[128,512]{1,0:T(8,128)S(1)}, f32[128,512]{1,0:T(8,128)}, u32[]{:S(2)}) copy-start(f32[128,512]{1,0:T(8,128)} %get-tuple-element.10.skipped_ref) | copy-start | bytes 786436

commit v2 on v1

--- a/solution.py
+++ b/solution.py
@@ -83,13 +83,7 @@
 
 
 def hops(places):
-    known, apart = [0], 1
-    steps = [[0]]
-    while apart < places:
-        steps.append([apart ^ step for step in known])
-        known = known + steps[-1]
-        apart *= 2
-    return steps
+    return [[apart, apart + 1] for apart in range(0, places, 2)]
 
 
 def prepare_kernel(
@@ -138,7 +132,7 @@
     features = features_in[...].astype(F32)
     scaled = (features * gain_in[...] * pre_in[...].astype(F32)).T
     pack(4, scaled.astype(BF16))
-    skipped_out[...] = scaled * skip_in[...].reshape(-1, 1)
+    skipped_out[...] = (scaled * skip_in[...].reshape(-1, 1)).astype(BF16)
     leave(skipped_out, skipped_ref)
     turned = features.T
     squares_out[...] = jnp.sum(turned * turned, axis=0, keepdims=True)
@@ -274,7 +268,7 @@
 
 
 def finish_kernel(conv_ref, skipped_ref, scale_ref, post_ref, out_ref):
-    turned = conv_ref[...].astype(F32) + skipped_ref[...] * scale_ref[...]
+    turned = conv_ref[...].astype(F32) + skipped_ref[...].astype(F32) * scale_ref[...]
     out_ref[...] = (post_ref[...].astype(F32) * turned.T).astype(BF16)
 
 
@@ -309,7 +303,7 @@
         prepare_kernel,
         (
             shape((1, rows), F32),
-            shape((wide, rows), F32),
+            shape((wide, rows), BF16),
             shape((places, 5, width, rows) if piled else (5, wide, rows), BF16),
         ),
         10 * cells,
@@ -329,7 +323,7 @@
             pltpu.VMEM((1, wide), F32),
             pltpu.VMEM(spectrum.shape, F32),
             pltpu.VMEM((1, rows), F32),
-            pltpu.VMEM((wide, rows), F32),
+            pltpu.VMEM((wide, rows), BF16),
             pltpu.VMEM((5, places, width, rows) if piled else (5, wide, rows), BF16),
             pltpu.SemaphoreType.DMA((8,)),
             pltpu.SemaphoreType.DMA((7,)),
@@ -343,11 +337,8 @@
         functools.partial(scale_kernel, wide * groups), shape((1, rows), F32), 8 * rows, 32 * rows, squares, *others
     )
     if piled:
-        scales, apart = [scale], 1
-        while apart < places:
-            known = jnp.concatenate(scales) if len(scales) > 1 else scale
-            scales.append(swap(known, "seq", apart))
-            apart *= 2
+        near = jnp.concatenate([scale, swap(scale, "seq", 1)])
+        scales = [near] + [swap(near, "seq", steps[0]) for steps in hops(places)[1:]]
     else:
         scales = [jnp.repeat(lax.all_gather(scale, "seq", axis=0, tiled=True), width, axis=0)]
         response = gathered[:, :4].reshape(places, 2, 2, width, rows).transpose(1, 0, 2, 3, 4)

time: 41.8 us -> 40.8 us (0.976)
  waiting for transfers between devices: 8.35 us -> 9.48 us
  starting transfers between devices: 16.7 us -> 15.6 us
  blocking collectives: 11.9 us -> 10.9 us
    ppermute x6 -> x7, waiting for transfers between devices: 8.35 us -> 9.47 us  [swap(): lax.ppermute(value, axis, [(place, place ^ apart) for place in range(lax....]
    ppermute x6 -> x7, starting transfers between devices: 9.24 us -> 8.13 us  [swap(): lax.ppermute(value, axis, [(place, place ^ apart) for place in range(lax....]
    all_to_all x1, blocking collectives: 11.9 us -> 10.9 us  [exchange(): return lax.all_to_all(value, 'seq', split_axis=0, concat_axis=0, tiled=True)]
  transfers between devices with their start and end apart: 7 -> 8, of which waited for: 5 -> 5; matrix products, arithmetic and copies ran while one was open for 0% -> 0% of each run, Pallas kernels for 0% -> 0%
where the time goes in v2:
time: 40.8 us; the launch traced here: 40.5 us
  starting transfers between devices  15.6 us (38%)
  blocking collectives  10.9 us (27%)
  waiting for transfers between devices  9.48 us (23%)
  Pallas kernels  4.36 us (11%)
    all_to_all x1, blocking collectives, exchange(): return lax.all_to_all(value, 'seq', split_axis=0, concat_axis=0, tiled=True)  10.9 us
    ppermute x7, waiting for transfers between devices, swap(): lax.ppermute(value, axis, [(place, place ^ apart) for place in range(lax....  9.47 us
    ppermute x7, starting transfers between devices, swap(): lax.ppermute(value, axis, [(place, place ^ apart) for place in range(lax....  8.13 us
    all_to_all x1, starting transfers between devices, exchange(): return lax.all_to_all(value, 'seq', split_axis=0, concat_axis=0, tiled=True)  7.42 us
    pallas_call x4, Pallas kernels, call(): pl.pallas_call(kernel, out_shape=out_shape, compiler_params=pltpu.Compile...  4.36 us
  transfers between devices with their start and end apart: 8, of which 5 were waited for; matrix products, arithmetic and copies ran while one was open for 0% of the time, Pallas kernels for 0%

profile of v2, /device:TPU:0, one launch (start us, length us, event | category | flops | bytes accessed | tf_op | source)
XLA Modules:
  0.0 40.5 jit_solution(2957007686512101787)
XLA Ops:
  0.0 2.4 %shard_map.118 = (f32[1,512]{1,0:T(1,128)}, bf16[128,512]{1,0:T(8,128)(2,1)}, bf16[8,5,16,512]{3,2,1,0:T(8,128)(2,1)}) custom-call(bf16[512,128]{1,0:T(8,128)(2,1)} %features_ref.1, bf16[512,128]{1,0:T(8,128)(2,1)} %pre_ref.1, f32[1,128]{1,0:T(1,128)} %bitcast.6, f32[1,128]{1,0:T(1,128)} %bitcast.7, f32[2,2,512,128]{3,2,1,0:T(8,128)} %spectrum_ref.1), custom_call_target="tpu_custom_call" | custom-call | flops 655360 | bytes 2097152 | tf_op jit(solution)/shard_map/pallas_call | solution.py:276
  2.4 0.0 copy-start.2
  2.4 0.0 copy-start.3
  2.4 0.0 copy-start.4
  2.4 0.0 copy-start.5
  2.4 0.0 copy-start.6
  2.5 0.0 copy-start.7
  2.5 7.4 %all-to-all-start = ((bf16[8,5,16,512]{3,2,1,0:T(8,128)(2,1)}), bf16[8,5,16,512]{3,2,1,0:T(8,128)(2,1)S(1)}, u32[]{:S(2)}, u32[]{:S(2)}) async-start(bf16[8,5,16,512]{3,2,1,0:T(8,128)(2,1)} %get-tuple-element.8), calls=%async_computation | async-start | bytes 1310720 | tf_op jit(solution)/shard_map/all_to_all | solution.py:286
  9.9 0.0 copy-done.2
  9.9 0.7 %collective-permute-start.2 = (f32[1,512]{1,0:T(1,128)S(1)}, f32[1,512]{1,0:T(1,128)S(1)}, u32[]{:S(2)}, u32[]{:S(2)}) collective-permute-start(f32[1,512]{1,0:T(1,128)S(1)} %copy-done.2), channel_id=1, source_target_pairs={{0,3},{1,2},{2,1},{3,0},{4,7},{5,6},{6,5},{7,4},{8,11},{9,10},{10,... | collective-permute-start | bytes 6152 | tf_op jit(solution)/shard_map/ppermute | solution.py:290
  10.6 0.9 %collective-permute-start.1 = (f32[1,512]{1,0:T(1,128)S(1)}, f32[1,512]{1,0:T(1,128)S(1)}, u32[]{:S(2)}, u32[]{:S(2)}) collective-permute-start(f32[1,512]{1,0:T(1,128)S(1)} %copy-done.2), channel_id=1, source_target_pairs={{0,2},{1,3},{2,0},{3,1},{4,6},{5,7},{6,4},{7,5},{8,10},{9,11},{10,... | collective-permute-start | bytes 6152 | tf_op jit(solution)/shard_map/ppermute | solution.py:290
  11.5 0.3 collective-permute-start
  11.8 1.1 %collective-permute-done.2.refs_3_ = f32[1,512]{1,0:T(1,128)S(1)} collective-permute-done((f32[1,512]{1,0:T(1,128)S(1)}, f32[1,512]{1,0:T(1,128)S(1)}, u32[]{:S(2)}, u32[]{:S(2)}) %collective-permute-start.2) | collective-permute-done | bytes 2080 | tf_op jit(solution)/shard_map/ppermute | solution.py:290
  13.0 1.2 %collective-permute-done.1.refs_2_ = f32[1,512]{1,0:T(1,128)S(1)} collective-permute-done((f32[1,512]{1,0:T(1,128)S(1)}, f32[1,512]{1,0:T(1,128)S(1)}, u32[]{:S(2)}, u32[]{:S(2)}) %collective-permute-start.1) | collective-permute-done | bytes 2080 | tf_op jit(solution)/shard_map/ppermute | solution.py:290
  14.2 0.0 collective-permute-done.refs_1_
  14.2 0.0 copy-start.8
  14.2 1.8 %collective-permute-start.3 = (f32[1,512]{1,0:T(1,128)S(1)}, f32[1,512]{1,0:T(1,128)S(1)}, u32[]{:S(2)}, u32[]{:S(2)}) collective-permute-start(f32[1,512]{1,0:T(1,128)S(1)} %shard_map.119.scale_ref), channel_id=1, source_target_pairs={{0,4},{4,0},{8,12},{12,8},{16,20},{20,16},{24,28},{28,24},{1,5},{5... | collective-permute-start | bytes 6152 | tf_op jit(solution)/shard_map/ppermute | solution.py:290
  16.0 1.9 %collective-permute-done.3 = f32[1,512]{1,0:T(1,128)S(1)} collective-permute-done((f32[1,512]{1,0:T(1,128)S(1)}, f32[1,512]{1,0:T(1,128)S(1)}, u32[]{:S(2)}, u32[]{:S(2)}) %collective-permute-start.3) | collective-permute-done | bytes 2080 | tf_op jit(solution)/shard_map/ppermute | solution.py:290
  17.9 3.7 %collective-permute-start.6 = (f32[2,512]{1,0:T(2,128)S(1)}, f32[2,512]{1,0:T(2,128)S(1)}, u32[]{:S(2)}, u32[]{:S(2)}) collective-permute-start(f32[2,512]{1,0:T(2,128)S(1)} %pad_maximum_fusion.refs_0_), channel_id=1, source_target_pairs={{0,24},{4,28},{8,16},{12,20},{16,8},{20,12},{24,0},{28,4},{1,25},{... | collective-permute-start | bytes 12296 | tf_op jit(solution)/shard_map/ppermute | solution.py:290
  21.6 0.0 collective-permute-start.5
  21.6 0.7 %collective-permute-start.4 = (f32[2,512]{1,0:T(2,128)S(1)}, f32[2,512]{1,0:T(2,128)S(1)}, u32[]{:S(2)}, u32[]{:S(2)}) collective-permute-start(f32[2,512]{1,0:T(2,128)S(1)} %pad_maximum_fusion.refs_0_), channel_id=1, source_target_pairs={{0,8},{4,12},{8,0},{12,4},{16,24},{20,28},{24,16},{28,20},{1,9},{5... | collective-permute-start | bytes 12296 | tf_op jit(solution)/shard_map/ppermute | solution.py:290
  22.4 2.4 %collective-permute-done.6.refs_3_ = f32[2,512]{1,0:T(2,128)S(1)} collective-permute-done((f32[2,512]{1,0:T(2,128)S(1)}, f32[2,512]{1,0:T(2,128)S(1)}, u32[]{:S(2)}, u32[]{:S(2)}) %collective-permute-start.6) | collective-permute-done | bytes 4128 | tf_op jit(solution)/shard_map/ppermute | solution.py:290
  24.8 2.8 %collective-permute-done.5.refs_2_ = f32[2,512]{1,0:T(2,128)S(1)} collective-permute-done((f32[2,512]{1,0:T(2,128)S(1)}, f32[2,512]{1,0:T(2,128)S(1)}, u32[]{:S(2)}, u32[]{:S(2)}) %collective-permute-start.5) | collective-permute-done | bytes 4128 | tf_op jit(solution)/shard_map/ppermute | solution.py:290
  27.5 0.0 collective-permute-done.4.refs_1_
  27.5 0.0 all-to-all-done.packed_ref
  27.5 0.0 copy-done.3
  27.6 0.0 copy-done.4
  27.6 1.2 %shard_map.120 = bf16[128,512]{1,0:T(8,128)(2,1)S(1)} custom-call(bf16[8,5,16,512]{3,2,1,0:T(8,128)(2,1)S(1)} %all-to-all-done.packed_ref, bf16[288,128]{1,0:T(8,128)(2,1)S(1)} %copy-done.5, bf16[128,288]{1,0:T(8,128)(2,1)S(1)} %copy-done.4, f32[2,9,512]{2,1,0:T(8,128)S(1)} %copy-done.6, f32[2,4,128]{2,1,0:T(4,128)S(1)} %copy-done.8, ...), custom_call_target="tpu_custom_call" | custom-call | flops 671088640 | bytes 1310720 | tf_op jit(solution)/shard_map/pallas_call | solution.py:276
  28.8 0.0 copy-start
  28.8 0.0 copy-start.1
  28.8 10.9 %all_to_all.10 = bf16[8,16,512]{2,1,0:T(8,128)(2,1)S(1)} all-to-all(bf16[8,16,512]{2,1,0:T(8,128)(2,1)S(1)} %bitcast.5), channel_id=1, replica_groups=mesh['seq'=8,'chan'=4] {'seq'}, dimensions={0} | all-to-all | bytes 262144 | tf_op jit(solution)/shard_map/all_to_all | solution.py:286
  39.7 0.8 %shard_map.121 = bf16[512,128]{1,0:T(8,128)(2,1)} custom-call(bf16[128,512]{1,0:T(8,128)(2,1)S(1)} %bitcast.4, bf16[128,512]{1,0:T(8,128)(2,1)S(1)} %copy-done.1, f32[1,512]{1,0:T(1,128)S(1)} %shard_map.119.scale_ref, bf16[512,128]{1,0:T(8,128)(2,1)S(1)} %copy-done), custom_call_target="tpu_custom_call" | custom-call | flops 655360 | bytes 524288 | tf_op jit(solution)/shard_map/pallas_call | solution.py:276
  (8 shorter events, 0.0 us)
Async XLA Ops:
  2.4 7.5 %copy-start.2 = (f32[1,512]{1,0:T(1,128)S(1)}, f32[1,512]{1,0:T(1,128)}, u32[]{:S(2)}) copy-start(f32[1,512]{1,0:T(1,128)} %get-tuple-element.9.refs_0_) | copy-start | bytes 6148
  2.4 25.1 %copy-start.3 = (bf16[2,256,256]{2,1,0:T(8,128)(2,1)S(1)}, bf16[2,256,256]{2,1,0:T(8,128)(2,1)}, u32[]{:S(2)}) copy-start(bf16[2,256,256]{2,1,0:T(8,128)(2,1)} %constant.16.clone.dft_ref) | copy-start | bytes 786436
  2.4 25.1 %copy-start.4 = (bf16[128,288]{1,0:T(8,128)(2,1)S(1)}, bf16[128,288]{1,0:T(8,128)(2,1)}, u32[]{:S(2)}) copy-start(bf16[128,288]{1,0:T(8,128)(2,1)} %constant.13.clone.last_ref) | copy-start | bytes 221188
  2.4 25.1 %copy-start.5 = (bf16[288,128]{1,0:T(8,128)(2,1)S(1)}, bf16[288,128]{1,0:T(8,128)(2,1)}, u32[]{:S(2)}) copy-start(bf16[288,128]{1,0:T(8,128)(2,1)} %constant.12.clone.first_ref) | copy-start | bytes 221188
  2.4 25.1 %copy-start.6 = (f32[2,9,512]{2,1,0:T(8,128)S(1)}, f32[2,9,512]{2,1,0:T(8,128)}, u32[]{:S(2)}) copy-start(f32[2,9,512]{2,1,0:T(8,128)} %constant.14.clone.twist_ref) | copy-start | bytes 110596
  2.5 25.1 %copy-start.7 = (bf16[128,128]{1,0:T(8,128)(2,1)S(1)}, bf16[128,128]{1,0:T(8,128)(2,1)}, u32[]{:S(2)}) copy-start(bf16[128,128]{1,0:T(8,128)(2,1)} %constant.17.clone.reverse_ref) | copy-start | bytes 98308
  2.5 25.1 %all-to-all-start = ((bf16[8,5,16,512]{3,2,1,0:T(8,128)(2,1)}), bf16[8,5,16,512]{3,2,1,0:T(8,128)(2,1)S(1)}, u32[]{:S(2)}, u32[]{:S(2)}) async-start(bf16[8,5,16,512]{3,2,1,0:T(8,128)(2,1)} %get-tuple-element.8), calls=%async_computation | async-start | bytes 1310720 | tf_op jit(solution)/shard_map/all_to_all | solution.py:286
  9.9 3.1 %collective-permute-start.2 = (f32[1,512]{1,0:T(1,128)S(1)}, f32[1,512]{1,0:T(1,128)S(1)}, u32[]{:S(2)}, u32[]{:S(2)}) collective-permute-start(f32[1,512]{1,0:T(1,128)S(1)} %copy-done.2), channel_id=1, source_target_pairs={{0,3},{1,2},{2,1},{3,0},{4,7},{5,6},{6,5},{7,4},{8,11},{9,10},{10,... | collective-permute-start | bytes 6152 | tf_op jit(solution)/shard_map/ppermute | solution.py:290
  10.6 3.6 %collective-permute-start.1 = (f32[1,512]{1,0:T(1,128)S(1)}, f32[1,512]{1,0:T(1,128)S(1)}, u32[]{:S(2)}, u32[]{:S(2)}) collective-permute-start(f32[1,512]{1,0:T(1,128)S(1)} %copy-done.2), channel_id=1, source_target_pairs={{0,2},{1,3},{2,0},{3,1},{4,6},{5,7},{6,4},{7,5},{8,10},{9,11},{10,... | collective-permute-start | bytes 6152 | tf_op jit(solution)/shard_map/ppermute | solution.py:290
  11.5 2.7 %collective-permute-start = (f32[1,512]{1,0:T(1,128)S(1)}, f32[1,512]{1,0:T(1,128)S(1)}, u32[]{:S(2)}, u32[]{:S(2)}) collective-permute-start(f32[1,512]{1,0:T(1,128)S(1)} %copy-done.2), channel_id=1, source_target_pairs={{0,1},{1,0},{2,3},{3,2},{4,5},{5,4},{6,7},{7,6},{8,9},{9,8},{10,11... | collective-permute-start | bytes 6152 | tf_op jit(solution)/shard_map/ppermute | solution.py:290
  14.2 13.4 %copy-start.8 = (f32[2,4,128]{2,1,0:T(4,128)S(1)}, f32[2,4,128]{2,1,0:T(4,128)}, u32[]{:S(2)}) copy-start(f32[2,4,128]{2,1,0:T(4,128)} %constant.15.clone.spin_ref) | copy-start | bytes 12292
  14.2 3.7 %collective-permute-start.3 = (f32[1,512]{1,0:T(1,128)S(1)}, f32[1,512]{1,0:T(1,128)S(1)}, u32[]{:S(2)}, u32[]{:S(2)}) collective-permute-start(f32[1,512]{1,0:T(1,128)S(1)} %shard_map.119.scale_ref), channel_id=1, source_target_pairs={{0,4},{4,0},{8,12},{12,8},{16,20},{20,16},{24,28},{28,24},{1,5},{5... | collective-permute-start | bytes 6152 | tf_op jit(solution)/shard_map/ppermute | solution.py:290
  17.9 6.8 %collective-permute-start.6 = (f32[2,512]{1,0:T(2,128)S(1)}, f32[2,512]{1,0:T(2,128)S(1)}, u32[]{:S(2)}, u32[]{:S(2)}) collective-permute-start(f32[2,512]{1,0:T(2,128)S(1)} %pad_maximum_fusion.refs_0_), channel_id=1, source_target_pairs={{0,24},{4,28},{8,16},{12,20},{16,8},{20,12},{24,0},{28,4},{1,25},{... | collective-permute-start | bytes 12296 | tf_op jit(solution)/shard_map/ppermute | solution.py:290
  21.6 5.9 %collective-permute-start.5 = (f32[2,512]{1,0:T(2,128)S(1)}, f32[2,512]{1,0:T(2,128)S(1)}, u32[]{:S(2)}, u32[]{:S(2)}) collective-permute-start(f32[2,512]{1,0:T(2,128)S(1)} %pad_maximum_fusion.refs_0_), channel_id=1, source_target_pairs={{0,16},{4,20},{8,24},{12,28},{16,0},{20,4},{24,8},{28,12},{1,17},{... | collective-permute-start | bytes 12296 | tf_op jit(solution)/shard_map/ppermute | solution.py:290
  21.6 5.9 %collective-permute-start.4 = (f32[2,512]{1,0:T(2,128)S(1)}, f32[2,512]{1,0:T(2,128)S(1)}, u32[]{:S(2)}, u32[]{:S(2)}) collective-permute-start(f32[2,512]{1,0:T(2,128)S(1)} %pad_maximum_fusion.refs_0_), channel_id=1, source_target_pairs={{0,8},{4,12},{8,0},{12,4},{16,24},{20,28},{24,16},{28,20},{1,9},{5... | collective-permute-start | bytes 12296 | tf_op jit(solution)/shard_map/ppermute | solution.py:290
  28.8 10.9 %copy-start = (bf16[512,128]{1,0:T(8,128)(2,1)S(1)}, bf16[512,128]{1,0:T(8,128)(2,1)}, u32[]{:S(2)}) copy-start(bf16[512,128]{1,0:T(8,128)(2,1)} %post_ref.1) | copy-start | bytes 393220
  28.8 10.9 %copy-start.1 = (bf16[128,512]{1,0:T(8,128)(2,1)S(1)}, bf16[128,512]{1,0:T(8,128)(2,1)}, u32[]{:S(2)}) copy-start(bf16[128,512]{1,0:T(8,128)(2,1)} %get-tuple-element.10.skipped_ref) | copy-start | bytes 393220

commit v3 on v2

--- a/solution.py
+++ b/solution.py
@@ -130,11 +130,11 @@
     for copy in arriving[:4]:
         copy.wait()
     features = features_in[...].astype(F32)
-    scaled = (features * gain_in[...] * pre_in[...].astype(F32)).T
-    pack(4, scaled.astype(BF16))
-    skipped_out[...] = (scaled * skip_in[...].reshape(-1, 1)).astype(BF16)
+    scaled = features * gain_in[...] * pre_in[...].astype(F32)
+    pack(4, scaled.astype(BF16).T)
+    skipped_out[...] = (scaled * skip_in[...]).astype(BF16).T
     leave(skipped_out, skipped_ref)
-    turned = features.T
+    turned = features_in[...].T.astype(F32)
     squares_out[...] = jnp.sum(turned * turned, axis=0, keepdims=True)
     leave(squares_out, squares_ref)
     for slot, block in enumerate(blocks):
@@ -142,9 +142,9 @@
         if len(packed_ref.shape) == 4:
             quarter = spectrum_in.shape[2] // 4
             rows = [spectrum_in[(*block, pl.ds(turn, quarter, stride=4), slice(None))] for turn in range(4)]
-            pack(slot, jnp.concatenate([row.T for row in rows], axis=1).astype(BF16))
+            pack(slot, jnp.concatenate([row.astype(BF16).T for row in rows], axis=1))
         else:
-            pack(slot, spectrum_in[block].T.astype(BF16))
+            pack(slot, spectrum_in[block].astype(BF16).T)
     for copy in leaving:
         copy.wait()
 

time: 40.8 us -> 40.7 us (level)
  no operation moved by 1% of the time
where the time goes in v3:
time: 40.7 us; the launch traced here: 40.4 us
  starting transfers between devices  15.6 us (38%)
  blocking collectives  10.9 us (27%)
  waiting for transfers between devices  9.48 us (23%)
  Pallas kernels  4.27 us (10%)
    all_to_all x1, blocking collectives, exchange(): return lax.all_to_all(value, 'seq', split_axis=0, concat_axis=0, tiled=True)  10.9 us
    ppermute x7, waiting for transfers between devices, swap(): lax.ppermute(value, axis, [(place, place ^ apart) for place in range(lax....  9.47 us
    ppermute x7, starting transfers between devices, swap(): lax.ppermute(value, axis, [(place, place ^ apart) for place in range(lax....  8.13 us
    all_to_all x1, starting transfers between devices, exchange(): return lax.all_to_all(value, 'seq', split_axis=0, concat_axis=0, tiled=True)  7.42 us
    pallas_call x4, Pallas kernels, call(): pl.pallas_call(kernel, out_shape=out_shape, compiler_params=pltpu.Compile...  4.27 us
  transfers between devices with their start and end apart: 8, of which 5 were waited for; matrix products, arithmetic and copies ran while one was open for 0% of the time, Pallas kernels for 0%

profile of v3, /device:TPU:0, one launch (start us, length us, event | category | flops | bytes accessed | tf_op | source)
XLA Modules:
  0.0 40.4 jit_solution(17164310352387977320)
XLA Ops:
  0.0 2.3 %shard_map.118 = (f32[1,512]{1,0:T(1,128)}, bf16[128,512]{1,0:T(8,128)(2,1)}, bf16[8,5,16,512]{3,2,1,0:T(8,128)(2,1)}) custom-call(bf16[512,128]{1,0:T(8,128)(2,1)} %features_ref.1, bf16[512,128]{1,0:T(8,128)(2,1)} %pre_ref.1, f32[1,128]{1,0:T(1,128)} %bitcast.6, f32[1,128]{1,0:T(1,128)} %bitcast.7, f32[2,2,512,128]{3,2,1,0:T(8,128)} %spectrum_ref.1), custom_call_target="tpu_custom_call" | custom-call | flops 655360 | bytes 2097152 | tf_op jit(solution)/shard_map/pallas_call | solution.py:276
  2.3 0.0 copy-start.2
  2.3 0.0 copy-start.3
  2.3 0.0 copy-start.4
  2.3 0.0 copy-start.5
  2.3 0.0 copy-start.6
  2.4 0.0 copy-start.7
  2.4 7.4 %all-to-all-start = ((bf16[8,5,16,512]{3,2,1,0:T(8,128)(2,1)}), bf16[8,5,16,512]{3,2,1,0:T(8,128)(2,1)S(1)}, u32[]{:S(2)}, u32[]{:S(2)}) async-start(bf16[8,5,16,512]{3,2,1,0:T(8,128)(2,1)} %get-tuple-element.8), calls=%async_computation | async-start | bytes 1310720 | tf_op jit(solution)/shard_map/all_to_all | solution.py:286
  9.8 0.0 copy-done.2
  9.8 0.7 %collective-permute-start.2 = (f32[1,512]{1,0:T(1,128)S(1)}, f32[1,512]{1,0:T(1,128)S(1)}, u32[]{:S(2)}, u32[]{:S(2)}) collective-permute-start(f32[1,512]{1,0:T(1,128)S(1)} %copy-done.2), channel_id=1, source_target_pairs={{0,3},{1,2},{2,1},{3,0},{4,7},{5,6},{6,5},{7,4},{8,11},{9,10},{10,... | collective-permute-start | bytes 6152 | tf_op jit(solution)/shard_map/ppermute | solution.py:290
  10.5 0.9 %collective-permute-start.1 = (f32[1,512]{1,0:T(1,128)S(1)}, f32[1,512]{1,0:T(1,128)S(1)}, u32[]{:S(2)}, u32[]{:S(2)}) collective-permute-start(f32[1,512]{1,0:T(1,128)S(1)} %copy-done.2), channel_id=1, source_target_pairs={{0,2},{1,3},{2,0},{3,1},{4,6},{5,7},{6,4},{7,5},{8,10},{9,11},{10,... | collective-permute-start | bytes 6152 | tf_op jit(solution)/shard_map/ppermute | solution.py:290
  11.4 0.3 collective-permute-start
  11.7 1.1 %collective-permute-done.2.refs_3_ = f32[1,512]{1,0:T(1,128)S(1)} collective-permute-done((f32[1,512]{1,0:T(1,128)S(1)}, f32[1,512]{1,0:T(1,128)S(1)}, u32[]{:S(2)}, u32[]{:S(2)}) %collective-permute-start.2) | collective-permute-done | bytes 2080 | tf_op jit(solution)/shard_map/ppermute | solution.py:290
  12.9 1.2 %collective-permute-done.1.refs_2_ = f32[1,512]{1,0:T(1,128)S(1)} collective-permute-done((f32[1,512]{1,0:T(1,128)S(1)}, f32[1,512]{1,0:T(1,128)S(1)}, u32[]{:S(2)}, u32[]{:S(2)}) %collective-permute-start.1) | collective-permute-done | bytes 2080 | tf_op jit(solution)/shard_map/ppermute | solution.py:290
  14.1 0.0 collective-permute-done.refs_1_
  14.1 0.0 copy-start.8
  14.1 1.8 %collective-permute-start.3 = (f32[1,512]{1,0:T(1,128)S(1)}, f32[1,512]{1,0:T(1,128)S(1)}, u32[]{:S(2)}, u32[]{:S(2)}) collective-permute-start(f32[1,512]{1,0:T(1,128)S(1)} %shard_map.119.scale_ref), channel_id=1, source_target_pairs={{0,4},{4,0},{8,12},{12,8},{16,20},{20,16},{24,28},{28,24},{1,5},{5... | collective-permute-start | bytes 6152 | tf_op jit(solution)/shard_map/ppermute | solution.py:290
  15.9 1.9 %collective-permute-done.3 = f32[1,512]{1,0:T(1,128)S(1)} collective-permute-done((f32[1,512]{1,0:T(1,128)S(1)}, f32[1,512]{1,0:T(1,128)S(1)}, u32[]{:S(2)}, u32[]{:S(2)}) %collective-permute-start.3) | collective-permute-done | bytes 2080 | tf_op jit(solution)/shard_map/ppermute | solution.py:290
  17.8 3.7 %collective-permute-start.6 = (f32[2,512]{1,0:T(2,128)S(1)}, f32[2,512]{1,0:T(2,128)S(1)}, u32[]{:S(2)}, u32[]{:S(2)}) collective-permute-start(f32[2,512]{1,0:T(2,128)S(1)} %pad_maximum_fusion.refs_0_), channel_id=1, source_target_pairs={{0,24},{4,28},{8,16},{12,20},{16,8},{20,12},{24,0},{28,4},{1,25},{... | collective-permute-start | bytes 12296 | tf_op jit(solution)/shard_map/ppermute | solution.py:290
  21.5 0.0 collective-permute-start.5
  21.6 0.7 %collective-permute-start.4 = (f32[2,512]{1,0:T(2,128)S(1)}, f32[2,512]{1,0:T(2,128)S(1)}, u32[]{:S(2)}, u32[]{:S(2)}) collective-permute-start(f32[2,512]{1,0:T(2,128)S(1)} %pad_maximum_fusion.refs_0_), channel_id=1, source_target_pairs={{0,8},{4,12},{8,0},{12,4},{16,24},{20,28},{24,16},{28,20},{1,9},{5... | collective-permute-start | bytes 12296 | tf_op jit(solution)/shard_map/ppermute | solution.py:290
  22.3 2.4 %collective-permute-done.6.refs_3_ = f32[2,512]{1,0:T(2,128)S(1)} collective-permute-done((f32[2,512]{1,0:T(2,128)S(1)}, f32[2,512]{1,0:T(2,128)S(1)}, u32[]{:S(2)}, u32[]{:S(2)}) %collective-permute-start.6) | collective-permute-done | bytes 4128 | tf_op jit(solution)/shard_map/ppermute | solution.py:290
  24.7 2.8 %collective-permute-done.5.refs_2_ = f32[2,512]{1,0:T(2,128)S(1)} collective-permute-done((f32[2,512]{1,0:T(2,128)S(1)}, f32[2,512]{1,0:T(2,128)S(1)}, u32[]{:S(2)}, u32[]{:S(2)}) %collective-permute-start.5) | collective-permute-done | bytes 4128 | tf_op jit(solution)/shard_map/ppermute | solution.py:290
  27.4 0.0 collective-permute-done.4.refs_1_
  27.4 0.0 all-to-all-done.packed_ref
  27.5 0.0 copy-done.3
  27.5 1.2 %shard_map.120 = bf16[128,512]{1,0:T(8,128)(2,1)S(1)} custom-call(bf16[8,5,16,512]{3,2,1,0:T(8,128)(2,1)S(1)} %all-to-all-done.packed_ref, bf16[288,128]{1,0:T(8,128)(2,1)S(1)} %copy-done.5, bf16[128,288]{1,0:T(8,128)(2,1)S(1)} %copy-done.4, f32[2,9,512]{2,1,0:T(8,128)S(1)} %copy-done.6, f32[2,4,128]{2,1,0:T(4,128)S(1)} %copy-done.8, ...), custom_call_target="tpu_custom_call" | custom-call | flops 671088640 | bytes 1310720 | tf_op jit(solution)/shard_map/pallas_call | solution.py:276
  28.7 0.0 copy-start
  28.7 0.0 copy-start.1
  28.7 10.9 %all_to_all.10 = bf16[8,16,512]{2,1,0:T(8,128)(2,1)S(1)} all-to-all(bf16[8,16,512]{2,1,0:T(8,128)(2,1)S(1)} %bitcast.5), channel_id=1, replica_groups=mesh['seq'=8,'chan'=4] {'seq'}, dimensions={0} | all-to-all | bytes 262144 | tf_op jit(solution)/shard_map/all_to_all | solution.py:286
  39.6 0.0 copy-done
  39.6 0.8 %shard_map.121 = bf16[512,128]{1,0:T(8,128)(2,1)} custom-call(bf16[128,512]{1,0:T(8,128)(2,1)S(1)} %bitcast.4, bf16[128,512]{1,0:T(8,128)(2,1)S(1)} %copy-done.1, f32[1,512]{1,0:T(1,128)S(1)} %shard_map.119.scale_ref, bf16[512,128]{1,0:T(8,128)(2,1)S(1)} %copy-done), custom_call_target="tpu_custom_call" | custom-call | flops 655360 | bytes 524288 | tf_op jit(solution)/shard_map/pallas_call | solution.py:276
  (8 shorter events, 0.0 us)
Async XLA Ops:
  2.3 7.5 %copy-start.2 = (f32[1,512]{1,0:T(1,128)S(1)}, f32[1,512]{1,0:T(1,128)}, u32[]{:S(2)}) copy-start(f32[1,512]{1,0:T(1,128)} %get-tuple-element.9.refs_0_) | copy-start | bytes 6148
  2.3 25.1 %copy-start.3 = (bf16[2,256,256]{2,1,0:T(8,128)(2,1)S(1)}, bf16[2,256,256]{2,1,0:T(8,128)(2,1)}, u32[]{:S(2)}) copy-start(bf16[2,256,256]{2,1,0:T(8,128)(2,1)} %constant.16.clone.dft_ref) | copy-start | bytes 786436
  2.3 25.1 %copy-start.4 = (bf16[128,288]{1,0:T(8,128)(2,1)S(1)}, bf16[128,288]{1,0:T(8,128)(2,1)}, u32[]{:S(2)}) copy-start(bf16[128,288]{1,0:T(8,128)(2,1)} %constant.13.clone.last_ref) | copy-start | bytes 221188
  2.3 25.1 %copy-start.5 = (bf16[288,128]{1,0:T(8,128)(2,1)S(1)}, bf16[288,128]{1,0:T(8,128)(2,1)}, u32[]{:S(2)}) copy-start(bf16[288,128]{1,0:T(8,128)(2,1)} %constant.12.clone.first_ref) | copy-start | bytes 221188
  2.3 25.1 %copy-start.6 = (f32[2,9,512]{2,1,0:T(8,128)S(1)}, f32[2,9,512]{2,1,0:T(8,128)}, u32[]{:S(2)}) copy-start(f32[2,9,512]{2,1,0:T(8,128)} %constant.14.clone.twist_ref) | copy-start | bytes 110596
  2.4 25.1 %copy-start.7 = (bf16[128,128]{1,0:T(8,128)(2,1)S(1)}, bf16[128,128]{1,0:T(8,128)(2,1)}, u32[]{:S(2)}) copy-start(bf16[128,128]{1,0:T(8,128)(2,1)} %constant.17.clone.reverse_ref) | copy-start | bytes 98308
  2.4 25.1 %all-to-all-start = ((bf16[8,5,16,512]{3,2,1,0:T(8,128)(2,1)}), bf16[8,5,16,512]{3,2,1,0:T(8,128)(2,1)S(1)}, u32[]{:S(2)}, u32[]{:S(2)}) async-start(bf16[8,5,16,512]{3,2,1,0:T(8,128)(2,1)} %get-tuple-element.8), calls=%async_computation | async-start | bytes 1310720 | tf_op jit(solution)/shard_map/all_to_all | solution.py:286
  9.8 3.1 %collective-permute-start.2 = (f32[1,512]{1,0:T(1,128)S(1)}, f32[1,512]{1,0:T(1,128)S(1)}, u32[]{:S(2)}, u32[]{:S(2)}) collective-permute-start(f32[1,512]{1,0:T(1,128)S(1)} %copy-done.2), channel_id=1, source_target_pairs={{0,3},{1,2},{2,1},{3,0},{4,7},{5,6},{6,5},{7,4},{8,11},{9,10},{10,... | collective-permute-start | bytes 6152 | tf_op jit(solution)/shard_map/ppermute | solution.py:290
  10.5 3.6 %collective-permute-start.1 = (f32[1,512]{1,0:T(1,128)S(1)}, f32[1,512]{1,0:T(1,128)S(1)}, u32[]{:S(2)}, u32[]{:S(2)}) collective-permute-start(f32[1,512]{1,0:T(1,128)S(1)} %copy-done.2), channel_id=1, source_target_pairs={{0,2},{1,3},{2,0},{3,1},{4,6},{5,7},{6,4},{7,5},{8,10},{9,11},{10,... | collective-permute-start | bytes 6152 | tf_op jit(solution)/shard_map/ppermute | solution.py:290
  11.4 2.7 %collective-permute-start = (f32[1,512]{1,0:T(1,128)S(1)}, f32[1,512]{1,0:T(1,128)S(1)}, u32[]{:S(2)}, u32[]{:S(2)}) collective-permute-start(f32[1,512]{1,0:T(1,128)S(1)} %copy-done.2), channel_id=1, source_target_pairs={{0,1},{1,0},{2,3},{3,2},{4,5},{5,4},{6,7},{7,6},{8,9},{9,8},{10,11... | collective-permute-start | bytes 6152 | tf_op jit(solution)/shard_map/ppermute | solution.py:290
  14.1 13.4 %copy-start.8 = (f32[2,4,128]{2,1,0:T(4,128)S(1)}, f32[2,4,128]{2,1,0:T(4,128)}, u32[]{:S(2)}) copy-start(f32[2,4,128]{2,1,0:T(4,128)} %constant.15.clone.spin_ref) | copy-start | bytes 12292
  14.1 3.7 %collective-permute-start.3 = (f32[1,512]{1,0:T(1,128)S(1)}, f32[1,512]{1,0:T(1,128)S(1)}, u32[]{:S(2)}, u32[]{:S(2)}) collective-permute-start(f32[1,512]{1,0:T(1,128)S(1)} %shard_map.119.scale_ref), channel_id=1, source_target_pairs={{0,4},{4,0},{8,12},{12,8},{16,20},{20,16},{24,28},{28,24},{1,5},{5... | collective-permute-start | bytes 6152 | tf_op jit(solution)/shard_map/ppermute | solution.py:290
  17.8 6.8 %collective-permute-start.6 = (f32[2,512]{1,0:T(2,128)S(1)}, f32[2,512]{1,0:T(2,128)S(1)}, u32[]{:S(2)}, u32[]{:S(2)}) collective-permute-start(f32[2,512]{1,0:T(2,128)S(1)} %pad_maximum_fusion.refs_0_), channel_id=1, source_target_pairs={{0,24},{4,28},{8,16},{12,20},{16,8},{20,12},{24,0},{28,4},{1,25},{... | collective-permute-start | bytes 12296 | tf_op jit(solution)/shard_map/ppermute | solution.py:290
  21.5 5.9 %collective-permute-start.5 = (f32[2,512]{1,0:T(2,128)S(1)}, f32[2,512]{1,0:T(2,128)S(1)}, u32[]{:S(2)}, u32[]{:S(2)}) collective-permute-start(f32[2,512]{1,0:T(2,128)S(1)} %pad_maximum_fusion.refs_0_), channel_id=1, source_target_pairs={{0,16},{4,20},{8,24},{12,28},{16,0},{20,4},{24,8},{28,12},{1,17},{... | collective-permute-start | bytes 12296 | tf_op jit(solution)/shard_map/ppermute | solution.py:290
  21.6 5.9 %collective-permute-start.4 = (f32[2,512]{1,0:T(2,128)S(1)}, f32[2,512]{1,0:T(2,128)S(1)}, u32[]{:S(2)}, u32[]{:S(2)}) collective-permute-start(f32[2,512]{1,0:T(2,128)S(1)} %pad_maximum_fusion.refs_0_), channel_id=1, source_target_pairs={{0,8},{4,12},{8,0},{12,4},{16,24},{20,28},{24,16},{28,20},{1,9},{5... | collective-permute-start | bytes 12296 | tf_op jit(solution)/shard_map/ppermute | solution.py:290
  28.7 10.9 %copy-start = (bf16[512,128]{1,0:T(8,128)(2,1)S(1)}, bf16[512,128]{1,0:T(8,128)(2,1)}, u32[]{:S(2)}) copy-start(bf16[512,128]{1,0:T(8,128)(2,1)} %post_ref.1) | copy-start | bytes 393220
  28.7 10.9 %copy-start.1 = (bf16[128,512]{1,0:T(8,128)(2,1)S(1)}, bf16[128,512]{1,0:T(8,128)(2,1)}, u32[]{:S(2)}) copy-start(bf16[128,512]{1,0:T(8,128)(2,1)} %get-tuple-element.10.skipped_ref) | copy-start | bytes 393220
